TPU v7x, 256 devices: a whole 4x4x8 slice. The times are simulated.
256 devices in a mesh: shot: 16 (over y, x), recv: 16 (over z, core).
Axes of the slice: x: 4, y: 4, z: 8, core: 2. Of those that a mesh axis runs over, the one named last changes fastest.
Arguments:
- traces: bfloat16 [256, 2048, 128], P('shot', 'recv'), may hold values from -6 to 6
- source_ids: int32 [256], P('shot'), may hold values from 0 to 255, as said below
- taper_ids: int32 [256], P('shot'), may hold values from 0 to 3
- recv_jitter: float32 [2, 2048], replicated, may hold values from -1 to 1
- aperture: int32 [16, 5], replicated, may hold values from -1 to 63, as said below
Outputs:
- multiples: bfloat16 [2, 64, 256, 2048], P(None, None, 'shot', 'recv')
Inputs may be any that keep to these rules, and one draw needn't show every extreme that they name: `source_ids`: A permutation of the source numbers. Of the 16 gathers of one shot index at most 2 have numbers in one block of 16 consecutive numbers, and exactly 2 in some block. `aperture`: row j names strips of distinct tiles, each within 3 tiles of j (strip g lies in tile g // 4); entry 0 is a strip of tile j itself; used entries come first, then -1. Every row uses 2 or more entries, and some row uses all 5.
All inputs are finite; a program needn't handle non-finite values.
Results may differ from a plain program's by a relative error of at most 0.0067.
Values may be sent and summed in bfloat16 or wider, within the bound.
A program may use at most 64 MiB of HBM per device.

v0:
```python
import math

import jax
import jax.numpy as jnp
from jax import lax
from jax.sharding import PartitionSpec as P

FREQS = 64
STRIPS = 4
APER = 5
HALF = 3
TAPERS = 4


onset_parts = 8.0
lateral_jitter = 0.4
crossline_spread = 3.0
depth_units = 8.0
wave_units = 32.0


def shifted(value, axis, steps):
    count = lax.axis_size(axis)
    leading, last = (max(0, -steps), min(count, count - steps))
    return lax.ppermute(value, axis, [(source, source + steps) for source in range(leading, last)])


def taper_windows(length):
    samples = jnp.arange(length, dtype=jnp.float32)
    onsets = jnp.arange(TAPERS, dtype=jnp.float32)[:, None] * (length / onset_parts)
    ramp_value = jnp.clip((samples[None, :] - onsets) / (length / onset_parts), 0.0, 1.0)
    return 0.5 - 0.5 * jnp.cos(jnp.pi * ramp_value)


def dft_table(length, freq_count):
    samples = jnp.arange(length, dtype=jnp.int32)[:, None]
    freq_bins = jnp.arange(freq_count, dtype=jnp.int32)[None, :]
    phase_index = (2 * freq_bins + 1) * samples % (2 * length)
    phase_angle = jnp.pi * phase_index.astype(jnp.float32) / length
    norm_scale = 1.0 / math.sqrt(length)
    dft_values = jnp.concatenate([jnp.cos(phase_angle), -jnp.sin(phase_angle)], axis=1) * norm_scale
    return dft_values.astype(jnp.bfloat16)


def windowed_transform(trace_rows, taper_list):
    length = trace_rows.shape[2]
    windows = taper_windows(length)
    chosen = jnp.zeros((trace_rows.shape[0], length), jnp.float32)
    for taper_index in range(TAPERS):
        chosen = (
            chosen
            + (taper_list == taper_index).astype(jnp.float32)[:, None]
            * windows[taper_index][None, :]
        )
    windowed = (trace_rows.astype(jnp.float32) * chosen[:, None, :]).astype(jnp.bfloat16)
    flat_rows = windowed.reshape(-1, length)
    spectra = jnp.dot(flat_rows, dft_table(length, FREQS), preferred_element_type=jnp.float32)
    return spectra.astype(jnp.bfloat16).reshape(trace_rows.shape[0], trace_rows.shape[1], 2 * FREQS)


def green_block(jitter, strip_id, reader_tile, strip_width, tile_width, live_weight):
    strip_start = strip_id * strip_width
    tile_start = reader_tile * tile_width
    strip_jitter = lax.dynamic_slice_in_dim(jitter, strip_start, strip_width, 1)
    local_jitter = lax.dynamic_slice_in_dim(jitter, tile_start, tile_width, 1)
    strip_x = (strip_start + jnp.arange(strip_width, dtype=jnp.int32)).astype(
        jnp.float32
    ) + lateral_jitter * strip_jitter[0]
    strip_y = crossline_spread * strip_jitter[1]
    local_x = (tile_start + jnp.arange(tile_width, dtype=jnp.int32)).astype(
        jnp.float32
    ) + lateral_jitter * local_jitter[0]
    local_y = crossline_spread * local_jitter[1]
    delta_x = strip_x[:, None] - local_x[None, :]
    delta_y = strip_y[:, None] - local_y[None, :]
    offset = jnp.sqrt(delta_x * delta_x + delta_y * delta_y)
    distance = jnp.sqrt(offset * offset + depth_units * depth_units)
    reach_units = float((HALF + 1) * tile_width)
    amplitude = (
        jnp.cos(0.5 * jnp.pi * jnp.minimum(offset / reach_units, 1.0))
        * live_weight
        / math.sqrt(APER * strip_width)
    )
    freq_bins = jnp.arange(FREQS, dtype=jnp.float32)[:, None, None] + 0.5
    phase = 2.0 * jnp.pi / wave_units * freq_bins * distance[None, :, :]
    real_part = amplitude[None, :, :] * jnp.cos(phase)
    imag_part = -amplitude[None, :, :] * jnp.sin(phase)
    from_real = jnp.stack([real_part, imag_part], axis=2)
    from_imag = jnp.stack([-imag_part, real_part], axis=2)
    green_values = jnp.stack([from_real, from_imag], axis=2)
    return green_values.reshape(FREQS, 2 * strip_width, 2 * tile_width).astype(jnp.bfloat16)


def local(traces, source_ids, taper_ids, recv_jitter, aperture):
    sources, tile_width, length = traces.shape
    shot_count = lax.axis_size("shot")
    capacity = 2 * sources // shot_count
    owner_tile = source_ids // sources
    within = source_ids % sources
    owner_picks = (owner_tile[:, None] == jnp.arange(shot_count, dtype=jnp.int32)[None, :]).astype(
        jnp.int32
    )
    order_rank = jnp.sum(jnp.cumsum(owner_picks, axis=0) * owner_picks, axis=1) - 1
    outgoing = (
        jnp.zeros((shot_count, capacity) + traces.shape[1:], jnp.bfloat16)
        .at[owner_tile, order_rank]
        .set(traces)
    )
    labels = jnp.stack([within, taper_ids], axis=1)
    outgoing_labels = (
        jnp.full((shot_count, capacity, 2), sources, jnp.int32)
        .at[owner_tile, order_rank]
        .set(labels)
    )
    arrived, arrived_labels = (
        lax.all_to_all(outgoing, "shot", split_axis=0, concat_axis=0, tiled=True),
        lax.all_to_all(outgoing_labels, "shot", split_axis=0, concat_axis=0, tiled=True),
    )
    arrived = arrived.reshape((shot_count * capacity,) + traces.shape[1:])
    arrived_labels = arrived_labels.reshape(shot_count * capacity, 2)
    slot_ids = arrived_labels[:, 0]
    placed = (
        jnp.zeros((sources,) + traces.shape[1:], jnp.bfloat16)
        .at[slot_ids]
        .set(arrived, mode="drop")
    )
    placed_tapers = (
        jnp.zeros((sources,), jnp.int32).at[slot_ids].set(arrived_labels[:, 1], mode="drop")
    )
    spectra = windowed_transform(placed, placed_tapers)
    strip_width = tile_width // STRIPS
    spectral_panel = spectra.reshape(sources, tile_width, 2, FREQS).transpose(3, 0, 1, 2)
    spectral_panel = spectral_panel.reshape(FREQS, sources, STRIPS, 2 * strip_width)
    own_tile = lax.axis_index("recv")
    entries = aperture[own_tile]
    owner_tiles = jnp.where(entries >= 0, entries // STRIPS, own_tile)
    source_index = jnp.clip(owner_tiles - own_tile + HALF, 0, 2 * HALF)
    whole_blocks = {}
    for distance_key in range(-HALF, HALF + 1):
        if distance_key == 0:
            whole_blocks[0] = spectral_panel
        else:
            whole_blocks[distance_key] = shifted(spectral_panel, "recv", -distance_key)
    gathered_whole = jnp.stack(
        [whole_blocks[distance_key] for distance_key in range(-HALF, HALF + 1)], axis=0
    )
    strip_within = jnp.maximum(entries, 0) % STRIPS
    accumulated = jnp.zeros((FREQS, sources, 2 * tile_width), jnp.float32)
    for slot_index in range(APER):
        strip_id = entries[slot_index]
        live_weight = (strip_id >= 0).astype(jnp.float32)
        clipped_strip = jnp.maximum(strip_id, 0)
        tile_panel = lax.dynamic_index_in_dim(
            gathered_whole, source_index[slot_index], 0, keepdims=False
        )
        strip_data = lax.dynamic_index_in_dim(
            tile_panel, strip_within[slot_index], 2, keepdims=False
        )
        green_table = green_block(
            recv_jitter, clipped_strip, own_tile, strip_width, tile_width, live_weight
        )
        accumulated = accumulated + jnp.einsum(
            "fsx,fxy->fsy", strip_data, green_table, preferred_element_type=jnp.float32
        )
    result = accumulated.astype(jnp.bfloat16).reshape(FREQS, sources, 2, tile_width)
    return result.transpose(2, 0, 1, 3)


def solution(mesh):
    placed = (P("shot", "recv", None), P("shot"), P("shot"), P(), P())
    return jax.shard_map(
        local, mesh=mesh, in_specs=placed, out_specs=P(None, None, "shot", "recv"), check_vma=False
    )
```

profile of v0, /device:TPU:65, one launch (start us, length us, event | category | flops | bytes accessed | tf_op | source)
XLA Modules:
  0.0 241.3 jit_solution(8142342612010334788)
XLA Ops:
  0.0 0.7 fusion.55
  1.0 0.7 pad_add_fusion
  1.7 0.6 broadcast_in_dim.12
  2.3 2.1 scatter_fusion
  4.4 6.8 %all-to-all-start = ((s32[16,2,2]{2,1,0:T(2,128)}), s32[16,2,2]{2,1,0:T(2,128)S(1)}, u32[]{:S(2)}, u32[]{:S(2)}) async-start(s32[16,2,2]{2,1,0:T(2,128)} %scatter_fusion), calls=%async_computation | async-start | bytes 32768 | tf_op jit(solution)/shard_map/all_to_all | solution.py:117
  11.2 0.9 fusion.63
  12.1 0.6 fusion.65
  16.0 0.8 constant_dynamic-slice_fusion
  20.4 0.3 fusion.47
  20.6 0.7 constant_dynamic-slice_fusion.8
  21.3 0.4 fusion.53
  21.8 20.3 %fusion.30 = (bf16[64,32,1,128]{3,1,2,0:T(8,128)(2,1)}, bf16[64,32,1,128]{3,1,2,0:T(8,128)(2,1)}, bf16[64,32,1,128]{3,1,2,0:T(8,128)(2,1)}, bf16[64,32,1,128]{3,...) fusion(f32[32,128]{1,0:T(8,128)S(1)} %get-tuple-element.49, ...), kind=kLoop, calls=%fused_computation.54 | loop fusion | flops 9175040 | bytes 8110336 | tf_op jit(solution)/shard_map/convert.12
  42.6 1.5 pad_maximum_fusion.1
  44.2 1.5 pad_maximum_fusion.2
  45.8 1.5 maximum_bitcast_fusion.6
  47.3 1.3 broadcast_in_dim.14
  48.6 2.8 %scatter_fusion.1 = bf16[16,2,128,128]{3,2,1,0:T(8,128)(2,1)} fusion(bf16[16,2,128,128]{3,2,1,0:T(8,128)(2,1)} %broadcast_in_dim.14, s32[16]{0:T(128)S(1)} %fusion.58, bf16[16,128,128]{2,1,0:T(8,128)(2,1)S(1)} %copy-done.11), kind=kCustom, calls=%fused_computation.1 | custom fusion | bytes 1572992 | tf_op jit(solution)/shard_map/scatter | solution.py:107
  51.4 6.7 %all-to-all-start.1 = ((bf16[16,2,128,128]{3,2,1,0:T(8,128)(2,1)}), bf16[16,2,128,128]{3,2,1,0:T(8,128)(2,1)S(1)}, u32[]{:S(2)}, u32[]{:S(2)}) async-start(bf16[16,2,128,128]{3,2,1,0:T(8,128)(2,1)} %scatter_fusion.1), calls=%async_computation.1 | async-start | bytes 2097152 | tf_op jit(solution)/shard_map/all_to_all | solution.py:116
  58.0 3.1 %pad_maximum_fusion.3 = bf16[64,32,2,2,128]{4,1,3,0,2:T(8,128)(2,1)} fusion(bf16[64,32,1,2,128]{4,1,3,0,2:T(8,128)(2,1)} %get-tuple-element.15, bf16[64,32,1,2,128]{4,1,3,0,2:T(8,128)(2,1)} %get-tuple-element.14), kind=kLoop, calls=%fused_computation.8 | loop fusion | flops 1048576 | bytes 4194304 | tf_op jit(solution)/shard_map/stack | solution.py:90
  61.4 0.9 scatter_custom_fusion.3
  62.3 11.1 %all-to-all-done.1 = bf16[16,2,128,128]{3,2,1,0:T(8,128)(2,1)S(1)} async-done(((bf16[16,2,128,128]{3,2,1,0:T(8,128)(2,1)}), bf16[16,2,128,128]{3,2,1,0:T(8,128)(2,1)S(1)}, u32[]{:S(2)}, u32[]{:S(2)}) %all-to-all-start.1) | async-done | bytes 1048608 | tf_op jit(solution)/shard_map/all_to_all | solution.py:116
  73.4 1.0 copy-done.10
  74.5 3.6 %scatter_fusion.2 = bf16[16,128,128]{2,1,0:T(8,128)(2,1)S(1)} fusion(bf16[16,128,128]{2,1,0:T(8,128)(2,1)S(1)} %broadcast_in_dim.11, s32[32]{0:T(128)S(1)} %fusion.57, bf16[32,128,128]{2,1,0:T(8,128)(2,1)} %bitcast.154), kind=kCustom, calls=%fused_computation.2 | custom fusion | bytes 3145856 | tf_op jit(solution)/shard_map/scatter | solution.py:125
  78.2 0.4 convolution_convert_fusion
  78.8 0.9 copy.75
  79.7 2.8 %copy.58 = bf16[64,16,128,2]{0,1,3,2:T(8,128)(2,1)S(1)} copy(bf16[64,16,128,2]{2,1,0,3:T(8,128)(2,1)} %bitcast.155) | data formatting | bytes 1048576 | tf_op jit(solution)/shard_map/transpose | solution.py:132
  82.5 9.1 %collective-permute-start = (bf16[64,16,4,64]{0,1,3,2:T(8,128)(2,1)S(1)}, bf16[64,16,4,64]{0,1,3,2:T(8,128)(2,1)}, u32[]{:S(2)}, u32[]{:S(2)}) collective-permute-start(bf16[64,16,4,64]{0,1,3,2:T(8,128)(2,1)S(1)} %bitcast.147), channel_id=1, source_target_pairs={{0,3},{1,4},{2,5},{3,6},{4,7},{5,8},{6,9},{7,10},{8,11},{9,12},{10... | collective-permute-start | bytes 1572872 | tf_op jit(solution)/shard_map/ppermute | solution.py:25
  91.6 3.0 %maximum_bitcast_fusion.8 = (bf16[64,32,1,2,128]{4,1,3,0,2:T(8,128)(2,1)}, bf16[64,32,1,2,128]{4,1,3,0,2:T(8,128)(2,1)}) fusion(bf16[64,32,1,128]{3,1,2,0:T(8,128)(2,1)} %get-tuple-element.22, bf16[64,32,1,128]{3,1,2,0:T(8,128)(2,1)} %get-tuple-element.32, bf16[64,32,1,128]{3,1,2,0:T(8,128)(2,1)} %get-tuple-element.23), kind=kLoop, calls=%fused_computation.64 | loop fusion | flops 1048576 | bytes 3670016 | tf_op jit(solution)/shard_map/stack | solution.py:90
  94.6 2.6 %collective-permute-start.1 = (bf16[64,16,4,64]{0,1,3,2:T(8,128)(2,1)S(1)}, bf16[64,16,4,64]{0,1,3,2:T(8,128)(2,1)}, u32[]{:S(2)}, u32[]{:S(2)}) collective-permute-start(bf16[64,16,4,64]{0,1,3,2:T(8,128)(2,1)S(1)} %bitcast.148), channel_id=1, source_target_pairs={{0,2},{1,3},{2,4},{3,5},{4,6},{5,7},{6,8},{7,9},{8,10},{9,11},{10,... | collective-permute-start | bytes 1572872 | tf_op jit(solution)/shard_map/ppermute | solution.py:25
  97.3 0.7 fusion.66
  116.7 3.6 %copy.61 = bf16[64,32,2,2,128]{4,3,2,1,0:T(2,128)(2,1)} copy(bf16[64,32,2,2,128]{4,1,3,0,2:T(8,128)(2,1)S(1)} %pad_maximum_fusion) | data formatting | bytes 4194304 | tf_op jit(solution)/shard_map/stack | solution.py:90
  120.3 4.6 %convert_element_type.148 = bf16[64,64,256]{2,1,0:T(8,128)(2,1)} reshape(bf16[64,32,2,2,128]{4,3,2,1,0:T(2,128)(2,1)} %copy.61) | data formatting | bytes 4194304 | tf_op jit(solution)/shard_map/convert_element_type | solution.py:91
  124.9 3.6 %copy.63 = bf16[64,32,2,2,128]{4,3,2,1,0:T(2,128)(2,1)} copy(bf16[64,32,2,2,128]{4,1,3,0,2:T(8,128)(2,1)S(1)} %copy-done) | data formatting | bytes 4194304 | tf_op jit(solution)/shard_map/stack | solution.py:90
  128.5 4.5 %convert_element_type.152 = bf16[64,64,256]{2,1,0:T(8,128)(2,1)} reshape(bf16[64,32,2,2,128]{4,3,2,1,0:T(2,128)(2,1)} %copy.63) | data formatting | bytes 4194304 | tf_op jit(solution)/shard_map/convert_element_type | solution.py:91
  133.0 3.6 %copy.65 = bf16[64,32,2,2,128]{4,3,2,1,0:T(2,128)(2,1)} copy(bf16[64,32,2,2,128]{4,1,3,0,2:T(8,128)(2,1)S(1)} %copy-done.1) | data formatting | bytes 4194304 | tf_op jit(solution)/shard_map/stack | solution.py:90
  136.6 4.5 %convert_element_type.156 = bf16[64,64,256]{2,1,0:T(8,128)(2,1)} reshape(bf16[64,32,2,2,128]{4,3,2,1,0:T(2,128)(2,1)} %copy.65) | data formatting | bytes 4194304 | tf_op jit(solution)/shard_map/convert_element_type | solution.py:91
  141.1 3.6 %copy.67 = bf16[64,32,2,2,128]{4,3,2,1,0:T(2,128)(2,1)} copy(bf16[64,32,2,2,128]{4,1,3,0,2:T(8,128)(2,1)S(1)} %copy-done.2) | data formatting | bytes 4194304 | tf_op jit(solution)/shard_map/stack | solution.py:90
  144.7 4.6 %convert_element_type.160 = bf16[64,64,256]{2,1,0:T(8,128)(2,1)} reshape(bf16[64,32,2,2,128]{4,3,2,1,0:T(2,128)(2,1)} %copy.67) | data formatting | bytes 4194304 | tf_op jit(solution)/shard_map/convert_element_type | solution.py:91
  149.5 2.2 copy.69
  151.7 2.7 %convert_element_type.164 = bf16[64,64,256]{2,1,0:T(8,128)(2,1)} reshape(bf16[64,32,2,2,128]{4,3,2,1,0:T(2,128)(2,1)S(1)} %copy.69) | data formatting | bytes 4194304 | tf_op jit(solution)/shard_map/convert_element_type | solution.py:91
  154.4 1.9 collective-permute-start.2
  156.3 2.4 collective-permute-start.3
  158.7 2.6 %collective-permute-start.4 = (bf16[64,16,4,64]{0,1,3,2:T(8,128)(2,1)S(1)}, bf16[64,16,4,64]{0,1,3,2:T(8,128)(2,1)S(1)}, u32[]{:S(2)}, u32[]{:S(2)}) collective-permute-start(bf16[64,16,4,64]{0,1,3,2:T(8,128)(2,1)S(1)} %bitcast.151), channel_id=1, source_target_pairs={{2,0},{3,1},{4,2},{5,3},{6,4},{7,5},{8,6},{9,7},{10,8},{11,9},{12,... | collective-permute-start | bytes 1572872 | tf_op jit(solution)/shard_map/ppermute | solution.py:25
  161.4 2.1 collective-permute-start.5
  163.5 1.4 bitcast_dynamic-update-slice_fusion.5
  165.0 1.5 bitcast_dynamic-update-slice_fusion.4
  166.4 1.6 collective-permute-done.2
  168.5 13.2 %collective-permute-done.3 = bf16[64,16,4,64]{0,1,3,2:T(8,128)(2,1)S(1)} collective-permute-done((bf16[64,16,4,64]{0,1,3,2:T(8,128)(2,1)S(1)}, bf16[64,16,4,64]{0,1,3,2:T(8,128)(2,1)S(1)}, u32[]{:S(2)}, u32[]{:S(2)}) %collective-permute-start.3) | collective-permute-done | bytes 524320 | tf_op jit(solution)/shard_map/ppermute | solution.py:25
  182.0 3.9 %collective-permute-done.4 = bf16[64,16,4,64]{0,1,3,2:T(8,128)(2,1)S(1)} collective-permute-done((bf16[64,16,4,64]{0,1,3,2:T(8,128)(2,1)S(1)}, bf16[64,16,4,64]{0,1,3,2:T(8,128)(2,1)S(1)}, u32[]{:S(2)}, u32[]{:S(2)}) %collective-permute-start.4) | collective-permute-done | bytes 524320 | tf_op jit(solution)/shard_map/ppermute | solution.py:25
  186.1 44.2 %collective-permute-done.5 = bf16[64,16,4,64]{0,1,3,2:T(8,128)(2,1)S(1)} collective-permute-done((bf16[64,16,4,64]{0,1,3,2:T(8,128)(2,1)S(1)}, bf16[64,16,4,64]{0,1,3,2:T(8,128)(2,1)S(1)}, u32[]{:S(2)}, u32[]{:S(2)}) %collective-permute-start.5) | collective-permute-done | bytes 524320 | tf_op jit(solution)/shard_map/ppermute | solution.py:25
  230.9 1.1 copy.60
  232.0 0.4 copy.62
  232.3 0.4 copy.64
  232.7 0.4 copy.66
  233.1 0.4 copy.68
  233.5 1.5 fusion.36
  235.2 0.4 convolution_add_fusion.3
  235.6 1.2 copy-done.5
  236.8 0.4 convolution_add_fusion.2
  237.2 1.2 copy-done.6
  238.4 0.4 convolution_add_fusion.1
  238.8 1.2 copy-done.7
  240.0 0.4 fusion.1
  240.4 0.9 copy.77
  (61 shorter events, 3.9 us)
Async XLA Ops:
  4.4 46.9 %all-to-all-start = ((s32[16,2,2]{2,1,0:T(2,128)}), s32[16,2,2]{2,1,0:T(2,128)S(1)}, u32[]{:S(2)}, u32[]{:S(2)}) async-start(s32[16,2,2]{2,1,0:T(2,128)} %scatter_fusion), calls=%async_computation | async-start | bytes 32768 | tf_op jit(solution)/shard_map/all_to_all | solution.py:117
  45.8 2.8 %copy-start.11 = (bf16[16,128,128]{2,1,0:T(8,128)(2,1)S(1)}, bf16[16,128,128]{2,1,0:T(8,128)(2,1)}, u32[]{:S(2)}) copy-start(bf16[16,128,128]{2,1,0:T(8,128)(2,1)} %param.5) | copy-start | bytes 1572868
  51.4 22.0 %all-to-all-start.1 = ((bf16[16,2,128,128]{3,2,1,0:T(8,128)(2,1)}), bf16[16,2,128,128]{3,2,1,0:T(8,128)(2,1)S(1)}, u32[]{:S(2)}, u32[]{:S(2)}) async-start(bf16[16,2,128,128]{3,2,1,0:T(8,128)(2,1)} %scatter_fusion.1), calls=%async_computation.1 | async-start | bytes 2097152 | tf_op jit(solution)/shard_map/all_to_all | solution.py:116
  73.4 1.0 copy-start.10
  82.5 78.8 %collective-permute-start = (bf16[64,16,4,64]{0,1,3,2:T(8,128)(2,1)S(1)}, bf16[64,16,4,64]{0,1,3,2:T(8,128)(2,1)}, u32[]{:S(2)}, u32[]{:S(2)}) collective-permute-start(bf16[64,16,4,64]{0,1,3,2:T(8,128)(2,1)S(1)} %bitcast.147), channel_id=1, source_target_pairs={{0,3},{1,4},{2,5},{3,6},{4,7},{5,8},{6,9},{7,10},{8,11},{9,12},{10... | collective-permute-start | bytes 1572872 | tf_op jit(solution)/shard_map/ppermute | solution.py:25
  94.6 70.3 %collective-permute-start.1 = (bf16[64,16,4,64]{0,1,3,2:T(8,128)(2,1)S(1)}, bf16[64,16,4,64]{0,1,3,2:T(8,128)(2,1)}, u32[]{:S(2)}, u32[]{:S(2)}) collective-permute-start(bf16[64,16,4,64]{0,1,3,2:T(8,128)(2,1)S(1)} %bitcast.148), channel_id=1, source_target_pairs={{0,2},{1,3},{2,4},{3,5},{4,6},{5,7},{6,8},{7,9},{8,10},{9,11},{10,... | collective-permute-start | bytes 1572872 | tf_op jit(solution)/shard_map/ppermute | solution.py:25
  120.3 4.6 %copy-start = (bf16[64,32,2,2,128]{4,1,3,0,2:T(8,128)(2,1)S(1)}, bf16[64,32,2,2,128]{4,1,3,0,2:T(8,128)(2,1)}, u32[]{:S(2)}) copy-start(bf16[64,32,2,2,128]{4,1,3,0,2:T(8,128)(2,1)} %pad_maximum_fusion.1) | copy-start | bytes 6291460
  128.5 4.5 %copy-start.1 = (bf16[64,32,2,2,128]{4,1,3,0,2:T(8,128)(2,1)S(1)}, bf16[64,32,2,2,128]{4,1,3,0,2:T(8,128)(2,1)}, u32[]{:S(2)}) copy-start(bf16[64,32,2,2,128]{4,1,3,0,2:T(8,128)(2,1)} %pad_maximum_fusion.2) | copy-start | bytes 6291460
  136.6 4.5 %copy-start.2 = (bf16[64,32,2,2,128]{4,1,3,0,2:T(8,128)(2,1)S(1)}, bf16[64,32,2,2,128]{4,1,3,0,2:T(8,128)(2,1)}, u32[]{:S(2)}) copy-start(bf16[64,32,2,2,128]{4,1,3,0,2:T(8,128)(2,1)} %pad_maximum_fusion.3) | copy-start | bytes 6291460
  144.7 4.6 %copy-start.8 = (bf16[64,32,1,2,128]{4,1,3,0,2:T(8,128)(2,1)S(1)}, bf16[64,32,1,2,128]{4,1,3,0,2:T(8,128)(2,1)}, u32[]{:S(2)}) copy-start(bf16[64,32,1,2,128]{4,1,3,0,2:T(8,128)(2,1)} %get-tuple-element.12) | copy-start | bytes 3145732
  144.7 4.6 %copy-start.9 = (bf16[64,32,1,2,128]{4,1,3,0,2:T(8,128)(2,1)S(1)}, bf16[64,32,1,2,128]{4,1,3,0,2:T(8,128)(2,1)}, u32[]{:S(2)}) copy-start(bf16[64,32,1,2,128]{4,1,3,0,2:T(8,128)(2,1)} %get-tuple-element.13) | copy-start | bytes 3145732
  154.4 13.6 %collective-permute-start.2 = (bf16[64,16,4,64]{0,1,3,2:T(8,128)(2,1)S(1)}, bf16[64,16,4,64]{0,1,3,2:T(8,128)(2,1)S(1)}, u32[]{:S(2)}, u32[]{:S(2)}) collective-permute-start(bf16[64,16,4,64]{0,1,3,2:T(8,128)(2,1)S(1)} %bitcast.149), channel_id=1, source_target_pairs={{0,1},{1,2},{2,3},{3,4},{4,5},{5,6},{6,7},{7,8},{8,9},{9,10},{10,1... | collective-permute-start | bytes 1572872 | tf_op jit(solution)/shard_map/ppermute | solution.py:25
  156.3 25.4 %collective-permute-start.3 = (bf16[64,16,4,64]{0,1,3,2:T(8,128)(2,1)S(1)}, bf16[64,16,4,64]{0,1,3,2:T(8,128)(2,1)S(1)}, u32[]{:S(2)}, u32[]{:S(2)}) collective-permute-start(bf16[64,16,4,64]{0,1,3,2:T(8,128)(2,1)S(1)} %bitcast.150), channel_id=1, source_target_pairs={{1,0},{2,1},{3,2},{4,3},{5,4},{6,5},{7,6},{8,7},{9,8},{10,9},{11,1... | collective-permute-start | bytes 1572872 | tf_op jit(solution)/shard_map/ppermute | solution.py:25
  158.7 27.1 %collective-permute-start.4 = (bf16[64,16,4,64]{0,1,3,2:T(8,128)(2,1)S(1)}, bf16[64,16,4,64]{0,1,3,2:T(8,128)(2,1)S(1)}, u32[]{:S(2)}, u32[]{:S(2)}) collective-permute-start(bf16[64,16,4,64]{0,1,3,2:T(8,128)(2,1)S(1)} %bitcast.151), channel_id=1, source_target_pairs={{2,0},{3,1},{4,2},{5,3},{6,4},{7,5},{8,6},{9,7},{10,8},{11,9},{12,... | collective-permute-start | bytes 1572872 | tf_op jit(solution)/shard_map/ppermute | solution.py:25
  161.4 69.0 %collective-permute-start.5 = (bf16[64,16,4,64]{0,1,3,2:T(8,128)(2,1)S(1)}, bf16[64,16,4,64]{0,1,3,2:T(8,128)(2,1)S(1)}, u32[]{:S(2)}, u32[]{:S(2)}) collective-permute-start(bf16[64,16,4,64]{0,1,3,2:T(8,128)(2,1)S(1)} %bitcast.152), channel_id=1, source_target_pairs={{3,0},{4,1},{5,2},{6,3},{7,4},{8,5},{9,6},{10,7},{11,8},{12,9},{13... | collective-permute-start | bytes 1572872 | tf_op jit(solution)/shard_map/ppermute | solution.py:25
  230.6 2.9 %copy-start.3 = (bf16[64,64,256]{2,1,0:T(8,128)(2,1)S(1)}, bf16[64,64,256]{2,1,0:T(8,128)(2,1)}, u32[]{:S(2)}) copy-start(bf16[64,64,256]{2,1,0:T(8,128)(2,1)} %convert_element_type.148) | copy-start | bytes 6291460
  233.5 1.7 copy-start.4
  235.2 1.6 copy-start.5
  236.8 1.6 copy-start.6
  238.4 1.6 copy-start.7
where the time goes:
time: 244 us; the launch traced here: 241 us
  waiting for transfers between devices  74 us (30%)
  local copies, waits for them, and re-layouts  69.4 us (28%)
  other arithmetic  34.5 us (14%)
  starting transfers between devices  34.2 us (14%)
  between operations  25.7 us (11%)
  matrix products  3.43 us (1%)
    ppermute x6, waiting for transfers between devices, shifted(): lax.ppermute(value, axis, [(source, source + steps) for source in range(l...  62.9 us
    convert_element_type x5, local copies, waits for them, and re-layouts, green_block(): green_values.reshape(FREQS, 2 * strip_width, 2 * tile_width)  20.9 us
    ppermute x6, starting transfers between devices, shifted(): lax.ppermute(value, axis, [(source, source + steps) for source in range(l...  20.8 us
    another operation x1, other arithmetic  20.3 us
    another operation x5, local copies, waits for them, and re-layouts, green_block(): green_values = jnp.stack([from_real, from_imag], axis=2)  16.5 us
    another operation x10, other arithmetic, green_block(): green_values = jnp.stack([from_real, from_imag], axis=2)  11.5 us
    all_to_all x1, waiting for transfers between devices, local(): lax.all_to_all(outgoing, 'shot', split_axis=0, concat_axis=0, tiled=True)  11.1 us
    unnamed x33, local copies, waits for them, and re-layouts  9.7 us
  transfers between devices with their start and end apart: 8, of which 5 were waited for; matrix products, arithmetic and copies ran while one was open for 34% of the time, Pallas kernels for 0%

commit v1 on v0

v1 whole, which is shorter than its diff:
```python
import functools
import math

import jax
import jax.numpy as jnp
import numpy as np
from jax import lax
from jax.experimental import pallas as pl
from jax.experimental.pallas import tpu as pltpu
from jax.sharding import PartitionSpec as P

FREQS = 64
STRIPS = 4
APER = 5
HALF = 3
SRC = 16
TILE = 128
STRIP = 32
SLOTS = 2
QUADS = FREQS // 4
PER = 2
CHUNKS = QUADS // PER
DIRS = (-3, -2, -1, 1, 2, 3)
MESH = pl.DeviceIdType.MESH
F32, BF16, I32 = jnp.float32, jnp.bfloat16, jnp.int32


def sine(x):
    z = x * x
    total = jnp.full_like(x, 1.0 / 6227020800.0)
    for term in (-1.0 / 39916800.0, 1.0 / 362880.0, -1.0 / 5040.0, 1.0 / 120.0, -1.0 / 6.0, 1.0):
        total = total * z + term
    return total * x


def cosine(x):
    z = x * x
    total = jnp.full_like(x, 1.0 / 479001600.0)
    for term in (-1.0 / 3628800.0, 1.0 / 40320.0, -1.0 / 720.0, 1.0 / 24.0, -0.5, 1.0):
        total = total * z + term
    return total


def iota(shape, dim):
    return lax.broadcasted_iota(I32, shape, dim)


def choose(which, options, values):
    chosen = values[0]
    for option, value in zip(options[1:], values[1:]):
        chosen = jnp.where(which == option, value, chosen)
    return chosen


def plus(one, two):
    return one[0] * two[0] - one[1] * two[1], one[1] * two[0] + one[0] * two[1]


def kernel(
    shots, tiles, ids, tapers, aperture, jitter, traces, table, out,
    spec, strips, zsend, zrecv, base, state, turn, green, pick, place, lsend, lrecv, asend, arecv,
    zsend_sem, zrecv_sem, lsend_sem, lrecv_sem, asend_sem, arecv_sem,
):
    me = lax.axis_index("shot")
    tile = lax.axis_index("recv")
    barrier = pltpu.get_barrier_semaphore()

    def shot_peer(step):
        return lax.rem(me + step, shots)

    def recv_peer(step):
        return lax.rem(tile + step + tiles, tiles)

    for step in range(1, shots):
        pl.semaphore_signal(barrier, inc=1, device_id={"shot": shot_peer(step)}, device_id_type=MESH)
    for step in DIRS:
        pl.semaphore_signal(barrier, inc=1, device_id={"recv": recv_peer(step)}, device_id_type=MESH)

    taper = jnp.zeros((SRC, TILE), I32)
    for a in range(SRC):
        taper = jnp.where(iota((SRC, TILE), 0) == a, tapers[a], taper)
    ramp = (iota((SRC, TILE), 1) - taper * 16).astype(F32) * (1.0 / 16.0)
    ramp = sine(jnp.clip(ramp, 0.0, 1.0) * (0.5 * math.pi))
    chosen = ramp * ramp

    for a in range(SRC):
        windowed = (traces[a].astype(F32) * chosen[a : a + 1, :]).astype(BF16)
        spec[pl.ds(a, 2 * FREQS, stride=SRC), :] = lax.dot_general(
            table[...], windowed, (((1,), (1,)), ((), ())), preferred_element_type=F32
        )

    wants = []
    for step in DIRS:
        reader = recv_peer(step)
        want = jnp.int32(0)
        for g in range(APER):
            entry = aperture[reader, g]
            want = jnp.where((entry >= 0) & ((entry >> 2) == tile), entry & 3, want)
        wants.append(want)

    row, lane = iota((SRC, TILE), 0), iota((SRC, TILE), 1)
    label = jnp.full((SRC, TILE), -1, I32)
    count = jnp.zeros((SRC, TILE), I32)
    for a in range(SRC):
        hit = row == (ids[a] >> 4)
        label = jnp.where(hit & (count == (lane & 1)), ids[a] & 15, label)
        count = count + hit.astype(I32)
    for t in range(SRC):
        lsend[t] = label[t : t + 1, :]

    pl.semaphore_wait(barrier, shots - 1 + len(DIRS))

    for step in range(1, shots):
        peer = shot_peer(step)
        pltpu.make_async_remote_copy(
            lsend.at[peer], lrecv.at[me], lsend_sem, lrecv_sem, device_id={"shot": peer}, device_id_type=MESH
        ).start()
    lrecv[me] = lsend[me]

    def send_strips(m, carry):
        for q in range(PER):
            quad = m * PER + q
            panel = spec[pl.ds(pl.multiple_of(quad * TILE, TILE), TILE), :].T.astype(BF16)
            strips[quad] = panel.reshape(STRIPS, STRIP, TILE)
            pieces = [strips[quad, s] for s in range(STRIPS)]
            for k in range(len(DIRS)):
                zsend[m, k, q] = choose(wants[k], range(STRIPS), pieces)
        for k, step in enumerate(DIRS):
            pltpu.make_async_remote_copy(
                zsend.at[m, k],
                zrecv.at[m, len(DIRS) - 1 - k],
                zsend_sem,
                zrecv_sem.at[m],
                device_id={"recv": recv_peer(step)},
                device_id_type=MESH,
            ).start()
        return carry

    lax.fori_loop(0, CHUNKS, send_strips, 0)

    lane = iota((8, TILE), 1)
    owner = jnp.zeros((8, TILE), I32)
    for a in range(SRC):
        owner = jnp.where((lane & 15) == a, ids[a] >> 4, owner)
    rank = jnp.zeros((8, TILE), I32)
    for a in range(SRC):
        rank = rank + ((owner == (ids[a] >> 4)) & ((lane & 15) > a)).astype(I32)
    shape = (SRC * 16, TILE)
    row, lane = iota(shape, 0), iota(shape, 1)
    same = (owner[:1] == (row >> 4)) & (rank[:1] == (row & 1)) & (((row >> 1) & 7) == (lane >> 4))
    pick[...] = same.astype(F32).astype(BF16)

    row, lane = iota((STRIP, TILE), 0), iota((STRIP, TILE), 1)
    here = pl.ds(pl.multiple_of(tile * TILE, TILE), TILE)
    local_x = (tile * TILE + lane).astype(F32) + 0.4 * jitter[0:1, here]
    local_y = 3.0 * jitter[1:2, here]
    near = range(-HALF, HALF + 1)
    jitters = [jitter[:, pl.ds(pl.multiple_of(recv_peer(step) * TILE, TILE), TILE)] for step in near]
    sources = []
    for g in range(APER):
        entry = aperture[tile, g]
        live = (entry >= 0).astype(F32)
        sources.append(jnp.where(entry >= 0, (entry >> 2) - tile, 0))
        strip = jnp.maximum(entry, 0)
        there = choose(sources[g], near, jitters)
        mask = lane == row + (strip & 3) * STRIP
        strip_x = jnp.sum(jnp.where(mask, there[0:1], 0.0), axis=1, keepdims=True)
        strip_y = jnp.sum(jnp.where(mask, there[1:2], 0.0), axis=1, keepdims=True)
        dx = (strip * STRIP + row).astype(F32) + 0.4 * strip_x - local_x
        dy = 3.0 * strip_y - local_y
        square = dx * dx + dy * dy
        cut = jnp.minimum(jnp.sqrt(square) * (1.0 / ((HALF + 1) * TILE)), 1.0)
        amp = cosine(cut * (0.5 * math.pi)) * (live / math.sqrt(APER * STRIP))
        turns = jnp.sqrt(square + 64.0) * (0.5 / 32.0)
        quarter = (turns - jnp.floor(turns + 0.5)) * math.pi
        sin_q, cos_q = sine(quarter), cosine(quarter)
        half = (1.0 - 2.0 * sin_q * sin_q, 2.0 * sin_q * cos_q)
        whole = plus(half, half)
        now = half
        for j in range(4):
            base[g, j, 0] = amp * now[0]
            base[g, j, 1] = amp * now[1]
            if j < 3:
                now = plus(now, whole)
        two = plus(whole, whole)
        four = plus(two, two)
        eight = plus(four, four)
        state[g, 0], state[g, 1] = four
        turn[g, 0], turn[g, 1] = eight

    own_strip = aperture[tile, 0] & 3

    def product(m, carry):
        for g in range(APER):
            rows = pl.ds(g * STRIP, STRIP)
            cos_a, sin_a = state[g, 0], state[g, 1]
            for j in range(4):
                cos_b, sin_b = base[g, j, 0], base[g, j, 1]
                cc, ss, sc, cs = cos_a * cos_b, sin_a * sin_b, sin_a * cos_b, cos_a * sin_b
                green[4 + j, rows, 0:TILE] = (cc - ss).astype(BF16)
                green[4 + j, rows, TILE : 2 * TILE] = (-sc - cs).astype(BF16)
                green[3 - j, rows, 0:TILE] = (cc + ss).astype(BF16)
                green[3 - j, rows, TILE : 2 * TILE] = (cs - sc).astype(BF16)
            state[g, 0], state[g, 1] = plus((cos_a, sin_a), (turn[g, 0], turn[g, 1]))

        pltpu.make_async_copy(zrecv.at[m], zrecv.at[m], zrecv_sem.at[m]).wait()
        panels = []
        for q in range(PER):
            arrived = [zrecv[m, k, q] for k in range(len(DIRS))]
            pieces = [choose(own_strip, range(STRIPS), [strips[m * PER + q, s] for s in range(STRIPS)])]
            for g in range(1, APER):
                pieces.append(choose(sources[g], DIRS, arrived))
            panel = jnp.concatenate(pieces, axis=0).T
            parts = []
            for f in range(4):
                both = jnp.dot(
                    panel[2 * SRC * f : 2 * SRC * (f + 1)], green[4 * q + f], preferred_element_type=F32
                )
                parts.append(both[:SRC, :TILE] - both[SRC:, TILE:])
                parts.append(both[:SRC, TILE:] + both[SRC:, :TILE])
            panels.append(jnp.concatenate(parts, axis=0).astype(BF16))
        slots = jnp.dot(pick[...], jnp.concatenate(panels, axis=1), preferred_element_type=F32).astype(BF16)
        for q in range(PER):
            asend[m, :, 16 * q : 16 * (q + 1), :] = slots[:, TILE * q : TILE * (q + 1)].reshape(SRC, 16, TILE)
        for step in range(1, shots):
            peer = shot_peer(step)
            pltpu.make_async_remote_copy(
                asend.at[m, peer],
                arecv.at[m, me],
                asend_sem,
                arecv_sem.at[m],
                device_id={"shot": peer},
                device_id_type=MESH,
            ).start()
        arecv[m, me] = asend[m, me]
        return carry

    lax.fori_loop(0, CHUNKS, product, 0)

    pltpu.make_async_copy(lrecv.at[pl.ds(0, shots - 1)], lrecv.at[pl.ds(0, shots - 1)], lrecv_sem).wait()
    row, lane = iota((TILE, TILE), 0), iota((TILE, TILE), 1)
    for h in range(2):
        label = jnp.zeros((1, TILE), I32)
        for j in range(8):
            label = jnp.where(iota((1, TILE), 1) >> 4 == j, lrecv[8 * h + j], label)
        same = (label == (row & 15)) & (((lane >> 2) & 3) == ((row >> 4) & 3)) & (((lane >> 1) & 1) == (row >> 6))
        place[:, TILE * h : TILE * (h + 1)] = same.astype(F32).astype(BF16)

    def finish(m, carry):
        part = arecv.at[m, pl.ds(0, shots - 1)]
        pltpu.make_async_copy(part, part, arecv_sem.at[m]).wait()
        blocks = [arecv[m, :, 16 * q : 16 * (q + 1), :].reshape(SRC * 16, TILE) for q in range(PER)]
        done = jnp.dot(place[...], jnp.concatenate(blocks, axis=1), preferred_element_type=F32).astype(BF16)
        for q in range(PER):
            for c in range(2):
                out[c, pl.ds((m * PER + q) * 4, 4)] = done[
                    64 * c : 64 * (c + 1), TILE * q : TILE * (q + 1)
                ].reshape(4, SRC, TILE)
        return carry

    lax.fori_loop(0, CHUNKS, finish, 0)

    pltpu.make_async_copy(zsend, zsend, zsend_sem).wait()
    part = lsend.at[pl.ds(0, shots - 1)]
    pltpu.make_async_copy(part, part, lsend_sem).wait()
    part = asend.at[:, pl.ds(0, shots - 1)]
    pltpu.make_async_copy(part, part, asend_sem).wait()


def dft_table():
    samples = np.arange(TILE)[None, :]
    bins = np.arange(FREQS)[:, None]
    angle = np.pi * ((2 * bins + 1) * samples % (2 * TILE)) / TILE
    values = np.stack([np.cos(angle), -np.sin(angle)], axis=1) / math.sqrt(TILE)
    return values.reshape(2 * FREQS, TILE)


def local(shots, tiles, traces, source_ids, taper_ids, recv_jitter, aperture):
    smem = pl.BlockSpec(memory_space=pltpu.SMEM)
    vmem = pl.BlockSpec(memory_space=pltpu.VMEM)
    table = jnp.asarray(dft_table(), BF16)
    dirs = len(DIRS)
    return pl.pallas_call(
        functools.partial(kernel, shots, tiles),
        out_shape=jax.ShapeDtypeStruct((2, FREQS, SRC, TILE), BF16),
        in_specs=[smem, smem, smem, vmem, vmem, vmem],
        out_specs=vmem,
        scratch_shapes=[
            pltpu.VMEM((2 * FREQS * SRC, TILE), F32),
            pltpu.VMEM((QUADS, STRIPS, STRIP, TILE), BF16),
            pltpu.VMEM((CHUNKS, dirs, PER, STRIP, TILE), BF16),
            pltpu.VMEM((CHUNKS, dirs, PER, STRIP, TILE), BF16),
            pltpu.VMEM((APER, 4, 2, STRIP, TILE), F32),
            pltpu.VMEM((APER, 2, STRIP, TILE), F32),
            pltpu.VMEM((APER, 2, STRIP, TILE), F32),
            pltpu.VMEM((4 * PER, APER * STRIP, 2 * TILE), BF16),
            pltpu.VMEM((SRC * 16, TILE), BF16),
            pltpu.VMEM((TILE, SRC * 16), BF16),
            pltpu.VMEM((SRC, 1, TILE), I32),
            pltpu.VMEM((SRC, 1, TILE), I32),
            pltpu.VMEM((CHUNKS, SRC, 16 * PER, TILE), BF16),
            pltpu.VMEM((CHUNKS, SRC, 16 * PER, TILE), BF16),
            pltpu.SemaphoreType.DMA,
            pltpu.SemaphoreType.DMA((CHUNKS,)),
            pltpu.SemaphoreType.DMA,
            pltpu.SemaphoreType.DMA,
            pltpu.SemaphoreType.DMA,
            pltpu.SemaphoreType.DMA((CHUNKS,)),
        ],
        compiler_params=pltpu.CompilerParams(
            collective_id=0, has_side_effects=True, vmem_limit_bytes=40 * 1024 * 1024
        ),
    )(source_ids, taper_ids, aperture, recv_jitter, traces, table)


def solution(mesh):
    placed = (P("shot", "recv", None), P("shot"), P("shot"), P(), P())
    return jax.shard_map(
        functools.partial(local, mesh.shape["shot"], mesh.shape["recv"]),
        mesh=mesh,
        in_specs=placed,
        out_specs=P(None, None, "shot", "recv"),
        check_vma=False,
    )
```

time: 244 us -> 34.3 us (0.14)
  the two profiles are of different devices: /device:TPU:65 before, /device:TPU:1 now
where the time goes in v1:
time: 34.3 us; the launch traced here: 34 us
  Pallas kernels  29.9 us (87%)
  local copies, waits for them, and re-layouts  4.11 us (12%)
    pallas_call x1, Pallas kernels, local(): pl.pallas_call(functools.partial(kernel, shots, tiles), out_shape=jax.Sha...  29.9 us
    unnamed x12, local copies, waits for them, and re-layouts  4.11 us

profile of v1, /device:TPU:1, one launch (start us, length us, event | category | flops | bytes accessed | tf_op | source)
XLA Modules:
  0.0 34.0 jit_solution(3371462124231846505)
XLA Ops:
  0.0 0.0 copy-start.4
  0.0 0.0 copy-start.3
  0.0 0.8 %copy.7.aperture = s32[16,5]{1,0:T(8,128)S(1)} copy(s32[16,5]{0,1:T(8,128)} %param.10) | data formatting | bytes 640 | tf_op args[4]
  0.8 0.0 copy-done.4
  0.8 0.0 copy-done.3
  0.8 0.0 copy-start
  0.8 1.0 %copy-done = bf16[16,128,128]{2,1,0:T(8,128)(2,1)S(1)} copy-done((bf16[16,128,128]{2,1,0:T(8,128)(2,1)S(1)}, bf16[16,128,128]{2,1,0:T(8,128)(2,1)}, u32[]{:S(2)}) %copy-start) | copy-done | bytes 524312
  1.8 0.0 copy-start.1
  1.8 0.8 %copy-done.1 = bf16[128,128]{1,0:T(8,128)(2,1)S(1)} copy-done((bf16[128,128]{1,0:T(8,128)(2,1)S(1)}, bf16[128,128]{1,0:T(8,128)(2,1)}, u32[]{:S(2)}) %copy-start.1) | copy-done | bytes 32792
  2.6 0.0 copy-start.2
  2.6 0.7 %copy-done.2 = f32[2,2048]{1,0:T(2,128)S(1)} copy-done((f32[2,2048]{1,0:T(2,128)S(1)}, f32[2,2048]{1,0:T(2,128)}, u32[]{:S(2)}) %copy-start.2) | copy-done | bytes 16408
  3.3 29.9 %shard_map.64 = bf16[2,64,16,128]{3,2,1,0:T(8,128)(2,1)S(1)} custom-call(s32[16]{0:T(128)S(1)} %copy-done.3, s32[16]{0:T(128)S(1)} %copy-done.4, s32[16,5]{1,0:T(8,128)S(1)} %copy.7.aperture, f32[2,2048]{1,0:T(2,128)S(1)} %copy-done.2, bf16[16,128,128]{2,1,0:T(8,128)(2,1)S(1)} %copy-done, bf16[128,128]{1,0:T(8,128)(2,1)S(1)} %copy-done.1), custom_call_target="tpu_custom_call" | custom-call | tf_op jit(solution)/shard_map/pallas_call | solution.py:283
  33.2 0.8 %copy.9 = bf16[2,64,16,128]{3,2,1,0:T(8,128)(2,1)} copy(bf16[2,64,16,128]{3,2,1,0:T(8,128)(2,1)S(1)} %shard_map.64) | data formatting | bytes 1048576
Async XLA Ops:
  0.0 0.8 %copy-start.4 = (s32[16]{0:T(128)S(1)}, s32[16]{0:T(128)}, u32[]{:S(2)}) copy-start(s32[16]{0:T(128)} %tapers.1) | copy-start | bytes 196
  0.0 0.8 %copy-start.3 = (s32[16]{0:T(128)S(1)}, s32[16]{0:T(128)}, u32[]{:S(2)}) copy-start(s32[16]{0:T(128)} %ids.1) | copy-start | bytes 196
  0.8 1.0 %copy-start = (bf16[16,128,128]{2,1,0:T(8,128)(2,1)S(1)}, bf16[16,128,128]{2,1,0:T(8,128)(2,1)}, u32[]{:S(2)}) copy-start(bf16[16,128,128]{2,1,0:T(8,128)(2,1)} %traces.1) | copy-start | bytes 1572868
  1.8 0.8 %copy-start.1 = (bf16[128,128]{1,0:T(8,128)(2,1)S(1)}, bf16[128,128]{1,0:T(8,128)(2,1)}, u32[]{:S(2)}) copy-start(bf16[128,128]{1,0:T(8,128)(2,1)} %constant.2.clone.table) | copy-start | bytes 98308
  2.6 0.7 %copy-start.2 = (f32[2,2048]{1,0:T(2,128)S(1)}, f32[2,2048]{1,0:T(2,128)}, u32[]{:S(2)}) copy-start(f32[2,2048]{1,0:T(2,128)} %jitter.1) | copy-start | bytes 49156

commit v2 on v1

v2 whole, which is shorter than its diff:
```python
import functools
import math

import jax
import jax.numpy as jnp
import numpy as np
from jax import lax
from jax.experimental import pallas as pl
from jax.experimental.pallas import tpu as pltpu
from jax.sharding import PartitionSpec as P

FREQS = 64
STRIPS = 4
APER = 5
HALF = 3
SRC = 16
TILE = 128
STRIP = 32
SLOTS = 2
QUADS = FREQS // 4
PER = 2
CHUNKS = QUADS // PER
LATE = 2
EARLY = CHUNKS - LATE
LEAD = 6
LOADS = 4
HOLD = 2
OFFSETS = sorted(
    ((dy, dx) for dy in range(4) for dx in range(4) if dy or dx),
    key=lambda o: -(min(o[0], 4 - o[0]) + min(o[1], 4 - o[1])),
)
DIRS = (-3, -2, -1, 1, 2, 3)
MESH = pl.DeviceIdType.MESH
F32, BF16, I32 = jnp.float32, jnp.bfloat16, jnp.int32


def sine(x):
    z = x * x
    total = jnp.full_like(x, 1.0 / 6227020800.0)
    for term in (-1.0 / 39916800.0, 1.0 / 362880.0, -1.0 / 5040.0, 1.0 / 120.0, -1.0 / 6.0, 1.0):
        total = total * z + term
    return total * x


def cosine(x):
    z = x * x
    total = jnp.full_like(x, 1.0 / 479001600.0)
    for term in (-1.0 / 3628800.0, 1.0 / 40320.0, -1.0 / 720.0, 1.0 / 24.0, -0.5, 1.0):
        total = total * z + term
    return total


def iota(shape, dim):
    return lax.broadcasted_iota(I32, shape, dim)


def choose(which, options, values):
    chosen = values[0]
    for option, value in zip(options[1:], values[1:]):
        chosen = jnp.where(which == option, value, chosen)
    return chosen


def plus(one, two):
    return one[0] * two[0] - one[1] * two[1], one[1] * two[0] + one[0] * two[1]


def kernel(
    tiles, ids_in, tapers_in, aperture_in, jitter_in, traces_in, table_in, out,
    ids, tapers, aperture, jitter, traces, table,
    spec, strips, zsend, zrecv, base, state, turn, green, pick, place, lsend, lrecv, asend, arecv,
    load_sem, zsend_sem, zrecv_sem, label_sem, asend_sem, arecv_sem,
):
    me = lax.axis_index("shot")
    tile = lax.axis_index("recv")
    my_y, my_x = me >> 2, me & 3
    barrier = pltpu.get_barrier_semaphore()

    def shot_peer(offset):
        return ((my_y + offset[0]) & 3) * 4 + ((my_x + offset[1]) & 3)

    def at_shot(peer):
        return {"device_id": {"shot": peer}, "device_id_type": MESH}

    def exists(step):
        return (tile + step >= 0) & (tile + step < tiles)

    loads = [
        pltpu.make_async_copy(ids_in, ids, load_sem.at[0]),
        pltpu.make_async_copy(tapers_in, tapers, load_sem.at[1]),
        pltpu.make_async_copy(aperture_in, aperture, load_sem.at[2]),
        pltpu.make_async_copy(jitter_in, jitter, load_sem.at[3]),
        pltpu.make_async_copy(table_in, table, load_sem.at[4]),
    ]
    part = SRC // LOADS
    for p in range(LOADS):
        rows = pl.ds(p * part, part)
        loads.append(pltpu.make_async_copy(traces_in.at[rows], traces.at[rows], load_sem.at[5 + p]))
    for load in loads:
        load.start()

    for offset in OFFSETS:
        pl.semaphore_signal(barrier, inc=1, **at_shot(shot_peer(offset)))
    peers = jnp.int32(len(OFFSETS))
    for step in DIRS:
        peers = peers + exists(step).astype(I32)

        @pl.when(exists(step))
        def _():
            pl.semaphore_signal(barrier, inc=1, device_id={"recv": tile + step}, device_id_type=MESH)

    for load in loads[:5]:
        load.wait()

    taper = jnp.zeros((SRC, TILE), I32)
    for a in range(SRC):
        taper = jnp.where(iota((SRC, TILE), 0) == a, tapers[a], taper)
    ramp = (iota((SRC, TILE), 1) - taper * 16).astype(F32) * (1.0 / 16.0)
    ramp = sine(jnp.clip(ramp, 0.0, 1.0) * (0.5 * math.pi))
    chosen = ramp * ramp

    lane = iota((8, TILE), 1)
    owner = jnp.zeros((8, TILE), I32)
    for a in range(SRC):
        owner = jnp.where((lane & 15) == a, ids[a] >> 4, owner)
    rank = jnp.zeros((8, TILE), I32)
    for a in range(SRC):
        rank = rank + ((owner == (ids[a] >> 4)) & ((lane & 15) > a)).astype(I32)
    shape = (SRC * 16, TILE)
    row, lane = iota(shape, 0), iota(shape, 1)
    same = (owner[:1] == (row >> 4)) & (rank[:1] == (row & 1)) & (((row >> 1) & 7) == (lane >> 4))
    pick[...] = same.astype(F32).astype(BF16)

    for a in range(SRC):
        if a % part == 0:
            loads[5 + a // part].wait()
        windowed = (traces[a].astype(F32) * chosen[a : a + 1, :]).astype(BF16)
        spec[pl.ds(a, 2 * FREQS, stride=SRC), :] = lax.dot_general(
            table[...], windowed, (((1,), (1,)), ((), ())), preferred_element_type=F32
        )

    wants = []
    for step in DIRS:
        reader = lax.rem(tile + step + tiles, tiles)
        want = jnp.int32(0)
        for g in range(APER):
            entry = aperture[g, reader]
            want = jnp.where((entry >= 0) & ((entry >> 2) == tile), entry & 3, want)
        wants.append(want)

    def split_strips(m, q, panel):
        quad = m * PER + q
        strips[quad] = panel.T.astype(BF16).reshape(STRIPS, STRIP, TILE)
        pieces = [strips[quad, s] for s in range(STRIPS)]
        for k in range(len(DIRS)):
            zsend[m, k, q] = choose(wants[k], range(STRIPS), pieces)

    def spec_panel(m, q):
        return spec[pl.ds(pl.multiple_of((m * PER + q) * TILE, TILE), TILE), :]

    def send_strips(m):
        for k, step in enumerate(DIRS):

            @pl.when(exists(step))
            def _():
                pltpu.make_async_remote_copy(
                    zsend.at[m, k],
                    zrecv.at[m, len(DIRS) - 1 - k],
                    zsend_sem.at[k],
                    zrecv_sem.at[m, len(DIRS) - 1 - k],
                    device_id={"recv": tile + step},
                    device_id_type=MESH,
                ).start()

    def early_strips(m):
        for q in range(PER):
            split_strips(m, q, spec_panel(m, q))
        send_strips(m)

    def send_rows(m, panels):
        slots = jnp.dot(pick[...], jnp.concatenate(panels, axis=1), preferred_element_type=F32).astype(BF16)
        for q in range(PER):
            asend[m, :, 16 * q : 16 * (q + 1), :] = slots[:, TILE * q : TILE * (q + 1)].reshape(SRC, 16, TILE)
        for offset in OFFSETS:
            peer = shot_peer(offset)
            pltpu.make_async_remote_copy(
                asend.at[m, peer], arecv.at[m, me], asend_sem, arecv_sem.at[m], **at_shot(peer)
            ).start()
        arecv[m, me] = asend[m, me]

    def placed_rows(m):
        most = arecv.at[m, pl.ds(0, SRC - 1)]
        pltpu.make_async_copy(most, most, arecv_sem.at[m]).wait()
        blocks = [arecv[m, :, 16 * q : 16 * (q + 1), :].reshape(SRC * 16, TILE) for q in range(PER)]
        rows = jnp.dot(place[...], jnp.concatenate(blocks, axis=1), preferred_element_type=F32)
        return [rows[:, TILE * q : TILE * (q + 1)] for q in range(PER)]

    for q in range(PER):
        split_strips(0, q, spec_panel(0, q))
    pl.semaphore_wait(barrier, peers)
    send_strips(0)
    for m in range(EARLY, CHUNKS):
        send_rows(m, [spec_panel(m, q).astype(BF16) for q in range(PER)])
    for m in range(1, LEAD):
        early_strips(m)

    row, lane = iota((SRC, TILE), 0), iota((SRC, TILE), 1)
    label = jnp.full((SRC, TILE), -1, I32)
    count = jnp.zeros((SRC, TILE), I32)
    for a in range(SRC):
        hit = row == (ids[a] >> 4)
        label = jnp.where(hit & (count == (lane & 1)), ids[a] & 15, label)
        count = count + hit.astype(I32)
    for t in range(SRC):
        lsend[t] = label[t : t + 1, :]
    lrecv[me] = lsend[me]
    for offset in OFFSETS:
        peer = shot_peer(offset)
        pltpu.make_async_remote_copy(
            lsend.at[peer], lrecv.at[me], label_sem.at[0], label_sem.at[1], **at_shot(peer)
        ).start()

    row, lane = iota((STRIP, TILE), 0), iota((STRIP, TILE), 1)
    here = pl.ds(pl.multiple_of(tile * TILE, TILE), TILE)
    local_x = (tile * TILE + lane).astype(F32) + 0.4 * jitter[0:1, here]
    local_y = 3.0 * jitter[1:2, here]
    near = (0,) + DIRS
    jitters = []
    for step in near:
        there = lax.rem(tile + step + tiles, tiles)
        jitters.append(jitter[:, pl.ds(pl.multiple_of(there * TILE, TILE), TILE)])
    sources = []
    for g in range(APER):
        entry = aperture[g, tile]
        live = (entry >= 0).astype(F32)
        sources.append(jnp.where(entry >= 0, (entry >> 2) - tile, 0))
        strip = jnp.maximum(entry, 0)
        there = choose(sources[g], near, jitters)
        mask = lane == row + (strip & 3) * STRIP
        strip_x = jnp.sum(jnp.where(mask, there[0:1], 0.0), axis=1, keepdims=True)
        strip_y = jnp.sum(jnp.where(mask, there[1:2], 0.0), axis=1, keepdims=True)
        dx = (strip * STRIP + row).astype(F32) + 0.4 * strip_x - local_x
        dy = 3.0 * strip_y - local_y
        square = dx * dx + dy * dy
        cut = jnp.minimum(jnp.sqrt(square) * (1.0 / ((HALF + 1) * TILE)), 1.0)
        amp = cosine(cut * (0.5 * math.pi)) * (live / math.sqrt(APER * STRIP))
        turns = jnp.sqrt(square + 64.0) * (0.5 / 32.0)
        quarter = (turns - jnp.floor(turns + 0.5)) * math.pi
        sin_q, cos_q = sine(quarter), cosine(quarter)
        half = (1.0 - 2.0 * sin_q * sin_q, 2.0 * sin_q * cos_q)
        whole = plus(half, half)
        now = half
        for j in range(4):
            base[g, j, 0] = amp * now[0]
            base[g, j, 1] = amp * now[1]
            if j < 3:
                now = plus(now, whole)
        two = plus(whole, whole)
        four = plus(two, two)
        eight = plus(four, four)
        state[g, 0], state[g, 1] = four
        turn[g, 0], turn[g, 1] = eight

    own_strip = aperture[0, tile] & 3

    def make_green():
        for g in range(APER):
            rows = pl.ds(g * STRIP, STRIP)
            cos_a, sin_a = state[g, 0], state[g, 1]
            for j in range(4):
                cos_b, sin_b = base[g, j, 0], base[g, j, 1]
                cc, ss, sc, cs = cos_a * cos_b, sin_a * sin_b, sin_a * cos_b, cos_a * sin_b
                green[4 + j, rows, 0:TILE] = (cc - ss).astype(BF16)
                green[4 + j, rows, TILE : 2 * TILE] = (-sc - cs).astype(BF16)
                green[3 - j, rows, 0:TILE] = (cc + ss).astype(BF16)
                green[3 - j, rows, TILE : 2 * TILE] = (cs - sc).astype(BF16)
            state[g, 0], state[g, 1] = plus((cos_a, sin_a), (turn[g, 0], turn[g, 1]))

    def product(m):
        for k, step in enumerate(DIRS):

            @pl.when(exists(step))
            def _():
                pltpu.make_async_copy(zrecv.at[m, k], zrecv.at[m, k], zrecv_sem.at[m, k]).wait()

        panels = []
        for q in range(PER):
            own = choose(own_strip, range(STRIPS), [strips[m * PER + q, s] for s in range(STRIPS)])
            pieces = [own]
            options = [own] + [zrecv[m, k, q] for k in range(len(DIRS))]
            for g in range(1, APER):
                pieces.append(choose(sources[g], near, options))
            panel = jnp.concatenate(pieces, axis=0).T
            parts = []
            for f in range(4):
                both = jnp.dot(
                    panel[2 * SRC * f : 2 * SRC * (f + 1)], green[4 * q + f], preferred_element_type=F32
                )
                parts.append(both[:SRC, :TILE] - both[SRC:, TILE:])
                parts.append(both[:SRC, TILE:] + both[SRC:, :TILE])
            panels.append(jnp.concatenate(parts, axis=0).astype(BF16))
        return panels

    def store(m, panels):
        for q in range(PER):
            panel = panels[q].astype(BF16).reshape(4, 2, SRC, TILE)
            for c in range(2):
                out[c, pl.ds((m * PER + q) * 4, 4)] = panel[:, c]

    def early(m, carry):
        @pl.when(m + LEAD < EARLY)
        def _():
            early_strips(m + LEAD)

        make_green()
        send_rows(m, product(m))
        return carry

    lax.fori_loop(0, EARLY, early, 0)

    most = lrecv.at[pl.ds(0, SRC - 1)]
    pltpu.make_async_copy(most, most, label_sem.at[1]).wait()
    row, lane = iota((TILE, TILE), 0), iota((TILE, TILE), 1)
    for h in range(2):
        label = jnp.zeros((1, TILE), I32)
        for j in range(8):
            label = jnp.where(iota((1, TILE), 1) >> 4 == j, lrecv[8 * h + j], label)
        same = (label == (row & 15)) & (((lane >> 1) & 7) == (row >> 4))
        place[:, TILE * h : TILE * (h + 1)] = same.astype(F32).astype(BF16)

    def relay(m, carry):
        rows = placed_rows(m)
        for q in range(PER):
            split_strips(m, q, rows[q])
        send_strips(m)
        return carry

    lax.fori_loop(EARLY, CHUNKS, relay, 0)

    def finish(m, carry):
        store(m, placed_rows(m))
        return carry

    lax.fori_loop(0, EARLY - HOLD, finish, 0)

    def late(m, carry):
        make_green()
        store(m, product(m))
        return carry

    lax.fori_loop(EARLY, CHUNKS, late, 0)
    lax.fori_loop(EARLY - HOLD, EARLY, finish, 0)

    for k, step in enumerate(DIRS):

        @pl.when(exists(step))
        def _():
            pltpu.make_async_copy(zsend.at[:, k], zsend.at[:, k], zsend_sem.at[k]).wait()

    most = lsend.at[pl.ds(0, SRC - 1)]
    pltpu.make_async_copy(most, most, label_sem.at[0]).wait()
    most = asend.at[:, pl.ds(0, SRC - 1)]
    pltpu.make_async_copy(most, most, asend_sem).wait()


def dft_table():
    samples = np.arange(TILE)[None, :]
    bins = np.arange(FREQS)[:, None]
    angle = np.pi * ((2 * bins + 1) * samples % (2 * TILE)) / TILE
    values = np.stack([np.cos(angle), -np.sin(angle)], axis=1) / math.sqrt(TILE)
    return values.reshape(2 * FREQS, TILE)


def local(tiles, traces, source_ids, taper_ids, recv_jitter, aperture):
    hbm = pl.BlockSpec(memory_space=pltpu.HBM)
    table = jnp.asarray(dft_table(), BF16)
    dirs = len(DIRS)
    return pl.pallas_call(
        functools.partial(kernel, tiles),
        out_shape=pltpu.VMEM((2, FREQS, SRC, TILE), BF16),
        in_specs=[hbm] * 6,
        out_specs=pl.BlockSpec(memory_space=pltpu.VMEM),
        scratch_shapes=[
            pltpu.SMEM((SRC,), I32),
            pltpu.SMEM((SRC,), I32),
            pltpu.SMEM((APER, tiles), I32),
            pltpu.VMEM(recv_jitter.shape, F32),
            pltpu.VMEM(traces.shape, BF16),
            pltpu.VMEM(table.shape, BF16),
            pltpu.VMEM((2 * FREQS * SRC, TILE), F32),
            pltpu.VMEM((QUADS, STRIPS, STRIP, TILE), BF16),
            pltpu.VMEM((CHUNKS, dirs, PER, STRIP, TILE), BF16),
            pltpu.VMEM((CHUNKS, dirs, PER, STRIP, TILE), BF16),
            pltpu.VMEM((APER, 4, 2, STRIP, TILE), F32),
            pltpu.VMEM((APER, 2, STRIP, TILE), F32),
            pltpu.VMEM((APER, 2, STRIP, TILE), F32),
            pltpu.VMEM((8, APER * STRIP, 2 * TILE), BF16),
            pltpu.VMEM((SRC * 16, TILE), BF16),
            pltpu.VMEM((TILE, SRC * 16), BF16),
            pltpu.VMEM((SRC, 1, TILE), I32),
            pltpu.VMEM((SRC, 1, TILE), I32),
            pltpu.VMEM((CHUNKS, SRC, 16 * PER, TILE), BF16),
            pltpu.VMEM((CHUNKS, SRC, 16 * PER, TILE), BF16),
            pltpu.SemaphoreType.DMA((5 + LOADS,)),
            pltpu.SemaphoreType.DMA((dirs,)),
            pltpu.SemaphoreType.DMA((CHUNKS, dirs)),
            pltpu.SemaphoreType.DMA((2,)),
            pltpu.SemaphoreType.DMA,
            pltpu.SemaphoreType.DMA((CHUNKS,)),
        ],
        compiler_params=pltpu.CompilerParams(
            collective_id=0, has_side_effects=True, vmem_limit_bytes=62 * 1024 * 1024
        ),
    )(source_ids, taper_ids, aperture.T, recv_jitter, traces, table)


def solution(mesh):
    placed = (P("shot", "recv", None), P("shot"), P("shot"), P(), P())
    return jax.shard_map(
        functools.partial(local, mesh.shape["recv"]),
        mesh=mesh,
        in_specs=placed,
        out_specs=P(None, None, "shot", "recv"),
        check_vma=False,
    )
```

time: 34.3 us -> 25 us (0.73)
  the two profiles are of different devices: /device:TPU:1 before, /device:TPU:33 now
where the time goes in v2:
time: 25 us; the launch traced here: 24.9 us
  Pallas kernels  24.1 us (96%)
  local copies, waits for them, and re-layouts  0.8 us (3%)
    pallas_call x1, Pallas kernels, local(): pl.pallas_call(functools.partial(kernel, tiles), out_shape=pltpu.VMEM((2,...  24.1 us
    unnamed x1, local copies, waits for them, and re-layouts  0.8 us

profile of v2, /device:TPU:33, one launch (start us, length us, event | category | flops | bytes accessed | tf_op | source)
XLA Modules:
  0.0 24.9 jit_solution(3661560561452484911)
XLA Ops:
  0.0 24.1 %shard_map.64 = bf16[2,64,16,128]{3,2,1,0:T(8,128)(2,1)S(1)} custom-call(s32[16]{0:T(128)} %ids_in.1, s32[16]{0:T(128)} %tapers_in.1, s32[5,16]{1,0:T(8,128)} %bitcast.1, f32[2,2048]{1,0:T(2,128)} %jitter_in.1, bf16[16,128,128]{2,1,0:T(8,128)(2,1)} %traces_in.1, bf16[128,128]{1,0:T(8,128)(2,1)} %constant.2.clone.table_in), custom_call_target="tpu_custom_call" | custom-call | tf_op jit(solution)/shard_map/pallas_call | solution.py:378
  24.1 0.8 %copy.8 = bf16[2,64,16,128]{3,2,1,0:T(8,128)(2,1)} copy(bf16[2,64,16,128]{3,2,1,0:T(8,128)(2,1)S(1)} %shard_map.64) | data formatting | bytes 1048576

commit v3 on v2

--- a/solution.py
+++ b/solution.py
@@ -20,16 +20,20 @@
 QUADS = FREQS // 4
 PER = 2
 CHUNKS = QUADS // PER
-LATE = 2
+LATE = 3
 EARLY = CHUNKS - LATE
-LEAD = 6
 LOADS = 4
 HOLD = 2
+SHIFT = 3
 OFFSETS = sorted(
     ((dy, dx) for dy in range(4) for dx in range(4) if dy or dx),
     key=lambda o: -(min(o[0], 4 - o[0]) + min(o[1], 4 - o[1])),
 )
 DIRS = (-3, -2, -1, 1, 2, 3)
+DEFER = (3,)
+ALL = range(len(DIRS))
+NOW = tuple(k for k in ALL if DIRS[k] not in DEFER)
+LATER = tuple(k for k in ALL if DIRS[k] in DEFER)
 MESH = pl.DeviceIdType.MESH
 F32, BF16, I32 = jnp.float32, jnp.bfloat16, jnp.int32
 
@@ -69,7 +73,7 @@
     tiles, ids_in, tapers_in, aperture_in, jitter_in, traces_in, table_in, out,
     ids, tapers, aperture, jitter, traces, table,
     spec, strips, zsend, zrecv, base, state, turn, green, pick, place, lsend, lrecv, asend, arecv,
-    load_sem, zsend_sem, zrecv_sem, label_sem, asend_sem, arecv_sem,
+    load_sem, zsend_sem, zrecv_sem, label_sem, asend_sem, arecv_sem, ready,
 ):
     me = lax.axis_index("shot")
     tile = lax.axis_index("recv")
@@ -82,8 +86,24 @@
     def at_shot(peer):
         return {"device_id": {"shot": peer}, "device_id_type": MESH}
 
+    def at_recv(step):
+        return {"device_id": {"recv": tile + step}, "device_id_type": MESH}
+
     def exists(step):
         return (tile + step >= 0) & (tile + step < tiles)
+
+    for offset in OFFSETS:
+        pl.semaphore_signal(barrier, inc=1, **at_shot(shot_peer(offset)))
+    peers = jnp.int32(len(OFFSETS))
+    for step in DIRS:
+        if step not in DEFER:
+            peers = peers + exists(step).astype(I32)
+        if -step in DEFER:
+            continue
+
+        @pl.when(exists(step))
+        def _():
+            pl.semaphore_signal(barrier, inc=1, **at_recv(step))
 
     loads = [
         pltpu.make_async_copy(ids_in, ids, load_sem.at[0]),
@@ -99,16 +119,6 @@
     for load in loads:
         load.start()
 
-    for offset in OFFSETS:
-        pl.semaphore_signal(barrier, inc=1, **at_shot(shot_peer(offset)))
-    peers = jnp.int32(len(OFFSETS))
-    for step in DIRS:
-        peers = peers + exists(step).astype(I32)
-
-        @pl.when(exists(step))
-        def _():
-            pl.semaphore_signal(barrier, inc=1, device_id={"recv": tile + step}, device_id_type=MESH)
-
     for load in loads[:5]:
         load.wait()
 
@@ -158,8 +168,9 @@
     def spec_panel(m, q):
         return spec[pl.ds(pl.multiple_of((m * PER + q) * TILE, TILE), TILE), :]
 
-    def send_strips(m):
-        for k, step in enumerate(DIRS):
+    def send_strips(m, which):
+        for k in which:
+            step = DIRS[k]
 
             @pl.when(exists(step))
             def _():
@@ -168,14 +179,8 @@
                     zrecv.at[m, len(DIRS) - 1 - k],
                     zsend_sem.at[k],
                     zrecv_sem.at[m, len(DIRS) - 1 - k],
-                    device_id={"recv": tile + step},
-                    device_id_type=MESH,
+                    **at_recv(step),
                 ).start()
-
-    def early_strips(m):
-        for q in range(PER):
-            split_strips(m, q, spec_panel(m, q))
-        send_strips(m)
 
     def send_rows(m, panels):
         slots = jnp.dot(pick[...], jnp.concatenate(panels, axis=1), preferred_element_type=F32).astype(BF16)
@@ -198,11 +203,19 @@
     for q in range(PER):
         split_strips(0, q, spec_panel(0, q))
     pl.semaphore_wait(barrier, peers)
-    send_strips(0)
+    for step in DEFER:
+
+        @pl.when(exists(-step))
+        def _():
+            pl.semaphore_signal(ready.at[step - 1], inc=1, **at_recv(-step))
+
+    send_strips(0, NOW)
     for m in range(EARLY, CHUNKS):
         send_rows(m, [spec_panel(m, q).astype(BF16) for q in range(PER)])
-    for m in range(1, LEAD):
-        early_strips(m)
+    for m in range(1, EARLY):
+        for q in range(PER):
+            split_strips(m, q, spec_panel(m, q))
+        send_strips(m, NOW)
 
     row, lane = iota((SRC, TILE), 0), iota((SRC, TILE), 1)
     label = jnp.full((SRC, TILE), -1, I32)
@@ -261,6 +274,15 @@
         state[g, 0], state[g, 1] = four
         turn[g, 0], turn[g, 1] = eight
 
+    for step in DEFER:
+
+        @pl.when(exists(step))
+        def _():
+            pl.semaphore_wait(ready.at[step - 1], 1)
+
+    for m in range(EARLY):
+        send_strips(m, LATER)
+
     own_strip = aperture[0, tile] & 3
 
     def make_green():
@@ -308,15 +330,11 @@
                 out[c, pl.ds((m * PER + q) * 4, 4)] = panel[:, c]
 
     def early(m, carry):
-        @pl.when(m + LEAD < EARLY)
-        def _():
-            early_strips(m + LEAD)
-
         make_green()
         send_rows(m, product(m))
         return carry
 
-    lax.fori_loop(0, EARLY, early, 0)
+    lax.fori_loop(0, SHIFT, early, 0)
 
     most = lrecv.at[pl.ds(0, SRC - 1)]
     pltpu.make_async_copy(most, most, label_sem.at[1]).wait()
@@ -332,10 +350,18 @@
         rows = placed_rows(m)
         for q in range(PER):
             split_strips(m, q, rows[q])
-        send_strips(m)
+        send_strips(m, ALL)
         return carry
 
-    lax.fori_loop(EARLY, CHUNKS, relay, 0)
+    def both(m, carry):
+        relay(EARLY - SHIFT + m, 0)
+        early(m, 0)
+        return carry
+
+    split = min(EARLY, SHIFT + LATE)
+    lax.fori_loop(SHIFT, split, both, 0)
+    lax.fori_loop(EARLY - SHIFT + split, CHUNKS, relay, 0)
+    lax.fori_loop(split, EARLY, early, 0)
 
     def finish(m, carry):
         store(m, placed_rows(m))
@@ -407,6 +433,7 @@
             pltpu.SemaphoreType.DMA((2,)),
             pltpu.SemaphoreType.DMA,
             pltpu.SemaphoreType.DMA((CHUNKS,)),
+            pltpu.SemaphoreType.REGULAR((HALF,)),
         ],
         compiler_params=pltpu.CompilerParams(
             collective_id=0, has_side_effects=True, vmem_limit_bytes=62 * 1024 * 1024

time: 25 us -> 24 us (0.960)
  the two profiles are of different devices: /device:TPU:33 before, /device:TPU:65 now
where the time goes in v3:
time: 24 us
  Pallas kernels  23.1 us (96%)
  local copies, waits for them, and re-layouts  0.8 us (3%)
    pallas_call x1, Pallas kernels, local(): pl.pallas_call(functools.partial(kernel, tiles), out_shape=pltpu.VMEM((2,...  23.1 us
    unnamed x1, local copies, waits for them, and re-layouts  0.8 us

profile of v3, /device:TPU:65, one launch (start us, length us, event | category | flops | bytes accessed | tf_op | source)
XLA Modules:
  0.0 24.0 jit_solution(14663262317561511097)
XLA Ops:
  0.0 23.1 %shard_map.64 = bf16[2,64,16,128]{3,2,1,0:T(8,128)(2,1)S(1)} custom-call(s32[16]{0:T(128)} %ids_in.1, s32[16]{0:T(128)} %tapers_in.1, s32[5,16]{1,0:T(8,128)} %bitcast.1, f32[2,2048]{1,0:T(2,128)} %jitter_in.1, bf16[16,128,128]{2,1,0:T(8,128)(2,1)} %traces_in.1, bf16[128,128]{1,0:T(8,128)(2,1)} %constant.2.clone.table_in), custom_call_target="tpu_custom_call" | custom-call | tf_op jit(solution)/shard_map/pallas_call | solution.py:404
  23.2 0.8 %copy.8 = bf16[2,64,16,128]{3,2,1,0:T(8,128)(2,1)} copy(bf16[2,64,16,128]{3,2,1,0:T(8,128)(2,1)S(1)} %shard_map.64) | data formatting | bytes 1048576

commit v4 on v3

--- a/solution.py
+++ b/solution.py
@@ -23,17 +23,16 @@
 LATE = 3
 EARLY = CHUNKS - LATE
 LOADS = 4
-HOLD = 2
+HOLD = 3
 SHIFT = 3
+EAGER = False
 OFFSETS = sorted(
     ((dy, dx) for dy in range(4) for dx in range(4) if dy or dx),
     key=lambda o: -(min(o[0], 4 - o[0]) + min(o[1], 4 - o[1])),
 )
 DIRS = (-3, -2, -1, 1, 2, 3)
-DEFER = (3,)
-ALL = range(len(DIRS))
-NOW = tuple(k for k in ALL if DIRS[k] not in DEFER)
-LATER = tuple(k for k in ALL if DIRS[k] in DEFER)
+GROUPS = ((0, 1), (1, 1), (2, 1), (3, 1), (4, 1))
+ALL, NEAR, FAR = range(6), range(5), range(5, 6)
 MESH = pl.DeviceIdType.MESH
 F32, BF16, I32 = jnp.float32, jnp.bfloat16, jnp.int32
 
@@ -72,8 +71,8 @@
 def kernel(
     tiles, ids_in, tapers_in, aperture_in, jitter_in, traces_in, table_in, out,
     ids, tapers, aperture, jitter, traces, table,
-    spec, strips, zsend, zrecv, base, state, turn, green, pick, place, lsend, lrecv, asend, arecv,
-    load_sem, zsend_sem, zrecv_sem, label_sem, asend_sem, arecv_sem, ready,
+    spec, strips, zsend, zrecv, base, state, turn, green, pick, place, lsend, lrecv, asend, arecv, bsend, brecv,
+    load_sem, zsend_sem, zrecv_sem, label_sem, asend_sem, arecv_sem, bsend_sem, brecv_sem, ready,
 ):
     me = lax.axis_index("shot")
     tile = lax.axis_index("recv")
@@ -94,14 +93,15 @@
 
     for offset in OFFSETS:
         pl.semaphore_signal(barrier, inc=1, **at_shot(shot_peer(offset)))
+    def slow(reader):
+        return (reader >= 4) & (reader < 11) & (reader % 2 == 0)
+
     peers = jnp.int32(len(OFFSETS))
     for step in DIRS:
-        if step not in DEFER:
-            peers = peers + exists(step).astype(I32)
-        if -step in DEFER:
-            continue
-
-        @pl.when(exists(step))
+        heard = exists(step) & jnp.logical_not(slow(tile + 3)) if step == 3 else exists(step)
+        peers = peers + heard.astype(I32)
+
+        @pl.when(exists(step) & jnp.logical_not(slow(tile)) if step == -3 else exists(step))
         def _():
             pl.semaphore_signal(barrier, inc=1, **at_recv(step))
 
@@ -168,54 +168,82 @@
     def spec_panel(m, q):
         return spec[pl.ds(pl.multiple_of((m * PER + q) * TILE, TILE), TILE), :]
 
-    def send_strips(m, which):
+    def send_strips(first, count, group, which):
+        chunks = pl.ds(first, count)
         for k in which:
             step = DIRS[k]
 
             @pl.when(exists(step))
             def _():
                 pltpu.make_async_remote_copy(
-                    zsend.at[m, k],
-                    zrecv.at[m, len(DIRS) - 1 - k],
+                    zsend.at[chunks, k],
+                    zrecv.at[chunks, len(DIRS) - 1 - k],
                     zsend_sem.at[k],
-                    zrecv_sem.at[m, len(DIRS) - 1 - k],
+                    zrecv_sem.at[group, len(DIRS) - 1 - k],
                     **at_recv(step),
                 ).start()
 
-    def send_rows(m, panels):
+    def wait_strips(first, count, group):
+        chunks = pl.ds(first, count)
+        for k, step in enumerate(DIRS):
+
+            @pl.when(exists(step))
+            def _():
+                pltpu.make_async_copy(zrecv.at[chunks, k], zrecv.at[chunks, k], zrecv_sem.at[group, k]).wait()
+
+    def lay_rows(panels):
         slots = jnp.dot(pick[...], jnp.concatenate(panels, axis=1), preferred_element_type=F32).astype(BF16)
-        for q in range(PER):
-            asend[m, :, 16 * q : 16 * (q + 1), :] = slots[:, TILE * q : TILE * (q + 1)].reshape(SRC, 16, TILE)
+        return [slots[:, TILE * q : TILE * (q + 1)].reshape(SRC, 16, TILE) for q in range(PER)]
+
+    def send_rows(first, count, group):
+        chunks = pl.ds(first, count)
         for offset in OFFSETS:
             peer = shot_peer(offset)
             pltpu.make_async_remote_copy(
-                asend.at[m, peer], arecv.at[m, me], asend_sem, arecv_sem.at[m], **at_shot(peer)
+                asend.at[chunks, peer], arecv.at[chunks, me], asend_sem, arecv_sem.at[group], **at_shot(peer)
             ).start()
-        arecv[m, me] = asend[m, me]
-
-    def placed_rows(m):
-        most = arecv.at[m, pl.ds(0, SRC - 1)]
-        pltpu.make_async_copy(most, most, arecv_sem.at[m]).wait()
-        blocks = [arecv[m, :, 16 * q : 16 * (q + 1), :].reshape(SRC * 16, TILE) for q in range(PER)]
+
+    def placed_rows(blocks):
         rows = jnp.dot(place[...], jnp.concatenate(blocks, axis=1), preferred_element_type=F32)
         return [rows[:, TILE * q : TILE * (q + 1)] for q in range(PER)]
 
+    def lay_late(late):
+        blocks = lay_rows([spec_panel(EARLY + late, q).astype(BF16) for q in range(PER)])
+        for q in range(PER):
+            first = 16 * (late * PER + q)
+            bsend[:, first : first + 16, :] = blocks[q]
+
     for q in range(PER):
         split_strips(0, q, spec_panel(0, q))
+    for late in range(LATE) if EAGER else ():
+        lay_late(late)
     pl.semaphore_wait(barrier, peers)
-    for step in DEFER:
-
-        @pl.when(exists(-step))
+
+    @pl.when(exists(-3) & slow(tile))
+    def _():
+        pl.semaphore_signal(ready, inc=1, **at_recv(-3))
+
+    def send_near(group):
+        first, count = GROUPS[group]
+        send_strips(first, count, group, NEAR)
+
+        @pl.when(jnp.logical_not(slow(tile + 3)))
         def _():
-            pl.semaphore_signal(ready.at[step - 1], inc=1, **at_recv(-step))
-
-    send_strips(0, NOW)
-    for m in range(EARLY, CHUNKS):
-        send_rows(m, [spec_panel(m, q).astype(BF16) for q in range(PER)])
-    for m in range(1, EARLY):
-        for q in range(PER):
-            split_strips(m, q, spec_panel(m, q))
-        send_strips(m, NOW)
+            send_strips(first, count, group, FAR)
+
+    send_near(0)
+    for late in range(LATE) if not EAGER else ():
+        lay_late(late)
+    for offset in OFFSETS:
+        peer = shot_peer(offset)
+        pltpu.make_async_remote_copy(bsend.at[peer], brecv.at[me], bsend_sem, brecv_sem, **at_shot(peer)).start()
+    brecv[me] = bsend[me]
+    for group in range(1, len(GROUPS)):
+        first, count = GROUPS[group]
+        for m in range(first, first + count):
+            for q in range(PER):
+                split_strips(m, q, spec_panel(m, q))
+        send_near(group)
 
     row, lane = iota((SRC, TILE), 0), iota((SRC, TILE), 1)
     label = jnp.full((SRC, TILE), -1, I32)
@@ -274,37 +302,31 @@
         state[g, 0], state[g, 1] = four
         turn[g, 0], turn[g, 1] = eight
 
-    for step in DEFER:
-
-        @pl.when(exists(step))
-        def _():
-            pl.semaphore_wait(ready.at[step - 1], 1)
-
-    for m in range(EARLY):
-        send_strips(m, LATER)
+    @pl.when(exists(3) & slow(tile + 3))
+    def _():
+        pl.semaphore_wait(ready, 1)
+        for group, (first, count) in enumerate(GROUPS):
+            send_strips(first, count, group, FAR)
 
     own_strip = aperture[0, tile] & 3
 
-    def make_green():
+    def make_green(m, carry):
         for g in range(APER):
             rows = pl.ds(g * STRIP, STRIP)
             cos_a, sin_a = state[g, 0], state[g, 1]
             for j in range(4):
                 cos_b, sin_b = base[g, j, 0], base[g, j, 1]
                 cc, ss, sc, cs = cos_a * cos_b, sin_a * sin_b, sin_a * cos_b, cos_a * sin_b
-                green[4 + j, rows, 0:TILE] = (cc - ss).astype(BF16)
-                green[4 + j, rows, TILE : 2 * TILE] = (-sc - cs).astype(BF16)
-                green[3 - j, rows, 0:TILE] = (cc + ss).astype(BF16)
-                green[3 - j, rows, TILE : 2 * TILE] = (cs - sc).astype(BF16)
+                green[m, 4 + j, rows, 0:TILE] = (cc - ss).astype(BF16)
+                green[m, 4 + j, rows, TILE : 2 * TILE] = (-sc - cs).astype(BF16)
+                green[m, 3 - j, rows, 0:TILE] = (cc + ss).astype(BF16)
+                green[m, 3 - j, rows, TILE : 2 * TILE] = (cs - sc).astype(BF16)
             state[g, 0], state[g, 1] = plus((cos_a, sin_a), (turn[g, 0], turn[g, 1]))
+        return carry
+
+    lax.fori_loop(0, EARLY, make_green, 0)
 
     def product(m):
-        for k, step in enumerate(DIRS):
-
-            @pl.when(exists(step))
-            def _():
-                pltpu.make_async_copy(zrecv.at[m, k], zrecv.at[m, k], zrecv_sem.at[m, k]).wait()
-
         panels = []
         for q in range(PER):
             own = choose(own_strip, range(STRIPS), [strips[m * PER + q, s] for s in range(STRIPS)])
@@ -316,7 +338,7 @@
             parts = []
             for f in range(4):
                 both = jnp.dot(
-                    panel[2 * SRC * f : 2 * SRC * (f + 1)], green[4 * q + f], preferred_element_type=F32
+                    panel[2 * SRC * f : 2 * SRC * (f + 1)], green[m, 4 * q + f], preferred_element_type=F32
                 )
                 parts.append(both[:SRC, :TILE] - both[SRC:, TILE:])
                 parts.append(both[:SRC, TILE:] + both[SRC:, :TILE])
@@ -330,11 +352,20 @@
                 out[c, pl.ds((m * PER + q) * 4, 4)] = panel[:, c]
 
     def early(m, carry):
-        make_green()
-        send_rows(m, product(m))
+        blocks = lay_rows(product(m))
+        for q in range(PER):
+            asend[m, :, 16 * q : 16 * (q + 1), :] = blocks[q]
+        arecv[m, me] = asend[m, me]
         return carry
 
-    lax.fori_loop(0, SHIFT, early, 0)
+    def early_group(group):
+        first, count = GROUPS[group]
+        wait_strips(first, count, group)
+        lax.fori_loop(first, first + count, early, 0)
+        send_rows(first, count, group)
+
+    for group in range(SHIFT):
+        early_group(group)
 
     most = lrecv.at[pl.ds(0, SRC - 1)]
     pltpu.make_async_copy(most, most, label_sem.at[1]).wait()
@@ -346,36 +377,45 @@
         same = (label == (row & 15)) & (((lane >> 1) & 7) == (row >> 4))
         place[:, TILE * h : TILE * (h + 1)] = same.astype(F32).astype(BF16)
 
+    most = brecv.at[pl.ds(0, SRC - 1)]
+    pltpu.make_async_copy(most, most, brecv_sem).wait()
+
     def relay(m, carry):
-        rows = placed_rows(m)
+        first = pl.multiple_of((m - EARLY) * PER * 16, PER * 16)
+        rows = brecv[:, pl.ds(first, PER * 16), :]
+        rows = placed_rows([rows[:, 16 * q : 16 * (q + 1)].reshape(SRC * 16, TILE) for q in range(PER)])
         for q in range(PER):
             split_strips(m, q, rows[q])
-        send_strips(m, ALL)
+        send_strips(m, 1, m - EARLY + len(GROUPS), ALL)
         return carry
 
-    def both(m, carry):
-        relay(EARLY - SHIFT + m, 0)
-        early(m, 0)
+    lax.fori_loop(EARLY, CHUNKS, relay, 0)
+    for group in range(SHIFT, len(GROUPS)):
+        early_group(group)
+
+    lax.fori_loop(EARLY, CHUNKS, make_green, 0)
+
+    def finish(m, carry):
+        store(m, placed_rows([arecv[m, :, 16 * q : 16 * (q + 1), :].reshape(SRC * 16, TILE) for q in range(PER)]))
         return carry
 
-    split = min(EARLY, SHIFT + LATE)
-    lax.fori_loop(SHIFT, split, both, 0)
-    lax.fori_loop(EARLY - SHIFT + split, CHUNKS, relay, 0)
-    lax.fori_loop(split, EARLY, early, 0)
-
-    def finish(m, carry):
-        store(m, placed_rows(m))
-        return carry
-
-    lax.fori_loop(0, EARLY - HOLD, finish, 0)
+    def finish_group(group):
+        first, count = GROUPS[group]
+        most = arecv.at[pl.ds(first, count), pl.ds(0, SRC - 1)]
+        pltpu.make_async_copy(most, most, arecv_sem.at[group]).wait()
+        lax.fori_loop(first, first + count, finish, 0)
+
+    for group in range(HOLD):
+        finish_group(group)
 
     def late(m, carry):
-        make_green()
+        wait_strips(m, 1, m - EARLY + len(GROUPS))
         store(m, product(m))
         return carry
 
     lax.fori_loop(EARLY, CHUNKS, late, 0)
-    lax.fori_loop(EARLY - HOLD, EARLY, finish, 0)
+    for group in range(HOLD, len(GROUPS)):
+        finish_group(group)
 
     for k, step in enumerate(DIRS):
 
@@ -387,6 +427,8 @@
     pltpu.make_async_copy(most, most, label_sem.at[0]).wait()
     most = asend.at[:, pl.ds(0, SRC - 1)]
     pltpu.make_async_copy(most, most, asend_sem).wait()
+    most = bsend.at[pl.ds(0, SRC - 1)]
+    pltpu.make_async_copy(most, most, bsend_sem).wait()
 
 
 def dft_table():
@@ -420,20 +462,24 @@
             pltpu.VMEM((APER, 4, 2, STRIP, TILE), F32),
             pltpu.VMEM((APER, 2, STRIP, TILE), F32),
             pltpu.VMEM((APER, 2, STRIP, TILE), F32),
-            pltpu.VMEM((8, APER * STRIP, 2 * TILE), BF16),
+            pltpu.VMEM((CHUNKS, 8, APER * STRIP, 2 * TILE), BF16),
             pltpu.VMEM((SRC * 16, TILE), BF16),
             pltpu.VMEM((TILE, SRC * 16), BF16),
             pltpu.VMEM((SRC, 1, TILE), I32),
             pltpu.VMEM((SRC, 1, TILE), I32),
-            pltpu.VMEM((CHUNKS, SRC, 16 * PER, TILE), BF16),
-            pltpu.VMEM((CHUNKS, SRC, 16 * PER, TILE), BF16),
+            pltpu.VMEM((EARLY, SRC, 16 * PER, TILE), BF16),
+            pltpu.VMEM((EARLY, SRC, 16 * PER, TILE), BF16),
+            pltpu.VMEM((SRC, LATE * 16 * PER, TILE), BF16),
+            pltpu.VMEM((SRC, LATE * 16 * PER, TILE), BF16),
             pltpu.SemaphoreType.DMA((5 + LOADS,)),
             pltpu.SemaphoreType.DMA((dirs,)),
-            pltpu.SemaphoreType.DMA((CHUNKS, dirs)),
+            pltpu.SemaphoreType.DMA((len(GROUPS) + LATE, dirs)),
             pltpu.SemaphoreType.DMA((2,)),
             pltpu.SemaphoreType.DMA,
-            pltpu.SemaphoreType.DMA((CHUNKS,)),
-            pltpu.SemaphoreType.REGULAR((HALF,)),
+            pltpu.SemaphoreType.DMA((len(GROUPS),)),
+            pltpu.SemaphoreType.DMA,
+            pltpu.SemaphoreType.DMA,
+            pltpu.SemaphoreType.REGULAR,
         ],
         compiler_params=pltpu.CompilerParams(
             collective_id=0, has_side_effects=True, vmem_limit_bytes=62 * 1024 * 1024

time: 24 us -> 23.4 us (0.975)
  Pallas kernels: 23.1 us -> 22.5 us
    pallas_call x1, Pallas kernels: 23.1 us -> 22.5 us  [local(): pl.pallas_call(functools.partial(kernel, tiles), out_shape=pltpu.VMEM((2,...]
where the time goes in v4:
time: 23.4 us; the launch traced here: 23.3 us
  Pallas kernels  22.5 us (96%)
  local copies, waits for them, and re-layouts  0.8 us (3%)
    pallas_call x1, Pallas kernels, local(): pl.pallas_call(functools.partial(kernel, tiles), out_shape=pltpu.VMEM((2,...  22.5 us
    unnamed x1, local copies, waits for them, and re-layouts  0.8 us

profile of v4, /device:TPU:65, one launch (start us, length us, event | category | flops | bytes accessed | tf_op | source)
XLA Modules:
  0.0 23.3 jit_solution(3738592544572571740)
XLA Ops:
  0.0 22.5 %shard_map.64 = bf16[2,64,16,128]{3,2,1,0:T(8,128)(2,1)S(1)} custom-call(s32[16]{0:T(128)} %ids_in.1, s32[16]{0:T(128)} %tapers_in.1, s32[5,16]{1,0:T(8,128)} %bitcast.1, f32[2,2048]{1,0:T(2,128)} %jitter_in.1, bf16[16,128,128]{2,1,0:T(8,128)(2,1)} %traces_in.1, bf16[128,128]{1,0:T(8,128)(2,1)} %constant.2.clone.table_in), custom_call_target="tpu_custom_call" | custom-call | tf_op jit(solution)/shard_map/pallas_call | solution.py:446
  22.5 0.8 %copy.8 = bf16[2,64,16,128]{3,2,1,0:T(8,128)(2,1)} copy(bf16[2,64,16,128]{3,2,1,0:T(8,128)(2,1)S(1)} %shard_map.64) | data formatting | bytes 1048576

commit v5 on v4

--- a/solution.py
+++ b/solution.py
@@ -25,7 +25,7 @@
 LOADS = 4
 HOLD = 3
 SHIFT = 3
-EAGER = False
+EAGER = True
 OFFSETS = sorted(
     ((dy, dx) for dy in range(4) for dx in range(4) if dy or dx),
     key=lambda o: -(min(o[0], 4 - o[0]) + min(o[1], 4 - o[1])),
@@ -94,7 +94,7 @@
     for offset in OFFSETS:
         pl.semaphore_signal(barrier, inc=1, **at_shot(shot_peer(offset)))
     def slow(reader):
-        return (reader >= 4) & (reader < 11) & (reader % 2 == 0)
+        return (reader >= 4) & (reader < 11)
 
     peers = jnp.int32(len(OFFSETS))
     for step in DIRS:
@@ -141,13 +141,15 @@
     same = (owner[:1] == (row >> 4)) & (rank[:1] == (row & 1)) & (((row >> 1) & 7) == (lane >> 4))
     pick[...] = same.astype(F32).astype(BF16)
 
-    for a in range(SRC):
+    for a in range(0, SRC, 2):
         if a % part == 0:
             loads[5 + a // part].wait()
-        windowed = (traces[a].astype(F32) * chosen[a : a + 1, :]).astype(BF16)
-        spec[pl.ds(a, 2 * FREQS, stride=SRC), :] = lax.dot_general(
-            table[...], windowed, (((1,), (1,)), ((), ())), preferred_element_type=F32
+        both = [(traces[b].astype(F32) * chosen[b : b + 1, :]).astype(BF16) for b in (a, a + 1)]
+        spectra = lax.dot_general(
+            table[...], jnp.concatenate(both, axis=0), (((1,), (1,)), ((), ())), preferred_element_type=F32
         )
+        for b in range(2):
+            spec[pl.ds(a + b, 2 * FREQS, stride=SRC), :] = spectra[:, TILE * b : TILE * (b + 1)]
 
     wants = []
     for step in DIRS:

time: 23.4 us -> 23.2 us (level)
  no operation moved by 1% of the time
where the time goes in v5:
time: 23.2 us; the launch traced here: 23.1 us
  Pallas kernels  22.3 us (96%)
  local copies, waits for them, and re-layouts  0.8 us (3%)
    pallas_call x1, Pallas kernels, local(): pl.pallas_call(functools.partial(kernel, tiles), out_shape=pltpu.VMEM((2,...  22.3 us
    unnamed x1, local copies, waits for them, and re-layouts  0.8 us

profile of v5, /device:TPU:65, one launch (start us, length us, event | category | flops | bytes accessed | tf_op | source)
XLA Modules:
  0.0 23.1 jit_solution(16338101042539855645)
XLA Ops:
  0.0 22.3 %shard_map.64 = bf16[2,64,16,128]{3,2,1,0:T(8,128)(2,1)S(1)} custom-call(s32[16]{0:T(128)} %ids_in.1, s32[16]{0:T(128)} %tapers_in.1, s32[5,16]{1,0:T(8,128)} %bitcast.1, f32[2,2048]{1,0:T(2,128)} %jitter_in.1, bf16[16,128,128]{2,1,0:T(8,128)(2,1)} %traces_in.1, bf16[128,128]{1,0:T(8,128)(2,1)} %constant.2.clone.table_in), custom_call_target="tpu_custom_call" | custom-call | tf_op jit(solution)/shard_map/pallas_call | solution.py:448
  22.3 0.8 %copy.8 = bf16[2,64,16,128]{3,2,1,0:T(8,128)(2,1)} copy(bf16[2,64,16,128]{3,2,1,0:T(8,128)(2,1)S(1)} %shard_map.64) | data formatting | bytes 1048576

commit v6 on v5

--- a/solution.py
+++ b/solution.py
@@ -238,7 +238,11 @@
         lay_late(late)
     for offset in OFFSETS:
         peer = shot_peer(offset)
-        pltpu.make_async_remote_copy(bsend.at[peer], brecv.at[me], bsend_sem, brecv_sem, **at_shot(peer)).start()
+        for late in range(LATE):
+            rows = pl.ds(late * PER * 16, PER * 16)
+            pltpu.make_async_remote_copy(
+                bsend.at[peer, rows], brecv.at[me, rows], bsend_sem, brecv_sem, **at_shot(peer)
+            ).start()
     brecv[me] = bsend[me]
     for group in range(1, len(GROUPS)):
         first, count = GROUPS[group]

time: 23.2 us -> 23.2 us (level)
  no operation moved by 1% of the time
where the time goes in v6:
time: 23.2 us; the launch traced here: 23.1 us
  Pallas kernels  22.3 us (96%)
  local copies, waits for them, and re-layouts  0.8 us (3%)
    pallas_call x1, Pallas kernels, local(): pl.pallas_call(functools.partial(kernel, tiles), out_shape=pltpu.VMEM((2,...  22.3 us
    unnamed x1, local copies, waits for them, and re-layouts  0.8 us

profile of v6, /device:TPU:65, one launch (start us, length us, event | category | flops | bytes accessed | tf_op | source)
XLA Modules:
  0.0 23.1 jit_solution(9989655526051218292)
XLA Ops:
  0.0 22.3 %shard_map.64 = bf16[2,64,16,128]{3,2,1,0:T(8,128)(2,1)S(1)} custom-call(s32[16]{0:T(128)} %ids_in.1, s32[16]{0:T(128)} %tapers_in.1, s32[5,16]{1,0:T(8,128)} %bitcast.1, f32[2,2048]{1,0:T(2,128)} %jitter_in.1, bf16[16,128,128]{2,1,0:T(8,128)(2,1)} %traces_in.1, bf16[128,128]{1,0:T(8,128)(2,1)} %constant.2.clone.table_in), custom_call_target="tpu_custom_call" | custom-call | tf_op jit(solution)/shard_map/pallas_call | solution.py:452
  22.3 0.8 %copy.8 = bf16[2,64,16,128]{3,2,1,0:T(8,128)(2,1)} copy(bf16[2,64,16,128]{3,2,1,0:T(8,128)(2,1)S(1)} %shard_map.64) | data formatting | bytes 1048576
